TPU v7x, 256 devices: a whole 4x4x8 slice. The times are simulated.
256 devices in a mesh: row: 128 (over z, y, x), rhs: 2 (over core).
Axes of the slice: x: 4, y: 4, z: 8, core: 2. Of those that a mesh axis runs over, the one named last changes fastest.
Arguments:
- source_field: float32 [2, 48, 131072], P(None, 'rhs', 'row'), may hold values from -6 to 6
- near_blocks: bfloat16 [512, 4, 2, 256, 256], P('row'), may hold values from -0.125 to 0.125
- near_offsets: int32 [512, 4], P('row'), may hold values from -2 to 2, as said below
- far_v: bfloat16 [16384, 2, 24, 256], P('row'), may hold values from -0.25 to 0.25
- far_u: bfloat16 [16384, 2, 24, 256], P('row', None, None, 'rhs'), may hold values from -0.109375 to 0.109375
- far_rank: int32 [16384], P('row'), may hold values from 8 to 24
- far_col_local: int32 [16384], P('row'), may hold values from 0 to 3
- far_dest: int32 [16384, 1], P('row'), may hold values from 0 to 127; in each aligned block of 128 rows (0 to 127, 128 to 255, ...) at most 2 rows name the same one
- far_row_local: int32 [16384], P('row'), may hold values from 0 to 3
Outputs:
- result: float32 [2, 48, 131072], P(None, 'rhs', 'row')
Inputs may be any that keep to these rules, and one draw needn't show every extreme that they name: `near_offsets`: offset 0 comes first for every cluster and a cluster's offsets are distinct; the first cluster of each index of row has an offset -2, the last one an offset 2. `far_dest`: among the 128 admissible blocks of one owner at most 2 name the same device; in every draw some owner has exactly 2 for one device.
All inputs are finite; a program needn't handle non-finite values.
Results may differ from a plain program's by a relative error of at most 0.011.
Values may be sent and summed in bfloat16 or wider, within the bound.
No kernel may reach another device: no remote copies, remote signals or barrier semaphores. Data moves between devices by JAX's collectives and lax.ppermute only.
A program may use at most 128 MiB of HBM per device.

v0:
```python
import jax
import jax.numpy as jnp
from jax import lax
from jax.sharding import PartitionSpec as P

APPS = 4


def padded_2(block, sides, width):
    for axis, dim in sides:
        count = lax.axis_size(axis)
        forward = [(i, i + 1) for i in range(count - 1)]
        backward = [(target, source) for source, target in forward]
        low = lax.ppermute(
            lax.slice_in_dim(block, block.shape[dim] - width, None, axis=dim), axis, forward
        )
        high = lax.ppermute(lax.slice_in_dim(block, 0, width, axis=dim), axis, backward)
        block = jnp.concatenate([low, block, high], axis=dim)
    return block


def on_device(
    source_field,
    near_blocks,
    near_offsets,
    far_v,
    far_u,
    far_rank,
    far_col_local,
    far_dest,
    far_row_local,
):
    parts_count, rhs_dev, panels_dev = source_field.shape
    clusters_dev, near_count, parts_two, leaf_size, leaf_again = near_blocks.shape
    far_count, parts_three, rank_size, leaf_third = far_v.shape
    rows_count = lax.axis_size("row")
    reach = clusters_dev // 2
    capacity = 2 * max(1, far_count // rows_count)
    slots_count = rows_count * capacity
    destination = far_dest[:, 0]
    ordinal = jnp.arange(far_count, dtype=jnp.int32)
    earlier = (destination[None, :] == destination[:, None]) & (ordinal[None, :] < ordinal[:, None])
    slot_id = destination * capacity + jnp.sum(earlier.astype(jnp.int32), axis=1)
    packer = jnp.arange(slots_count, dtype=jnp.int32)[:, None] == slot_id[None, :]
    packer_bf = packer.astype(jnp.bfloat16)
    row_slots = jnp.sum(packer.astype(jnp.int32) * far_row_local[None, :], axis=1).reshape(
        rows_count, capacity
    )

    def into_slots(values):
        flattened = values.reshape(far_count, -1)
        placed = jnp.dot(packer_bf, flattened, preferred_element_type=jnp.float32).astype(
            jnp.bfloat16
        )
        return placed.reshape((rows_count, capacity) + values.shape[1:])

    full_u = lax.all_gather(far_u, "rhs", axis=3, tiled=True)
    received_u, received_rows = (
        lax.all_to_all(into_slots(full_u), "row", split_axis=0, concat_axis=0, tiled=True),
        lax.all_to_all(row_slots, "row", split_axis=0, concat_axis=0, tiled=True),
    )
    received_u = received_u.reshape(slots_count, 2, rank_size, leaf_size)
    received_rows = received_rows.reshape(slots_count)
    spread = (jnp.arange(clusters_dev, dtype=jnp.int32)[:, None] == received_rows[None, :]).astype(
        jnp.bfloat16
    )
    owned = (jnp.arange(clusters_dev, dtype=jnp.int32)[None, :] == far_col_local[:, None]).astype(
        jnp.bfloat16
    )
    centre_ids = jnp.arange(clusters_dev, dtype=jnp.int32)[:, None] + near_offsets + reach
    choose = (
        jnp.arange(clusters_dev + 2 * reach, dtype=jnp.int32)[None, None, :]
        == centre_ids[:, :, None]
    ).astype(jnp.bfloat16)
    kept = (jnp.arange(rank_size, dtype=jnp.int32)[None, :] < far_rank[:, None])[:, :, None]
    current = source_field
    for application in range(APPS):
        rounded = current.astype(jnp.bfloat16)
        padded = padded_2(rounded, (("row", 2),), reach * leaf_size)
        padded = padded.reshape(2, rhs_dev, clusters_dev + 2 * reach, leaf_size)
        columns = jnp.einsum(
            "ikm,crml->ikcrl", choose, padded, preferred_element_type=jnp.float32
        ).astype(jnp.bfloat16)
        products = jnp.einsum(
            "ikapl,ikcrl->acrip", near_blocks, columns, preferred_element_type=jnp.float32
        )
        near_term = jnp.stack([products[0, 0] - products[1, 1], products[0, 1] + products[1, 0]])
        local_view = rounded.reshape(2, rhs_dev, clusters_dev, leaf_size)
        picked = jnp.einsum(
            "bm,crml->bcrl", owned, local_view, preferred_element_type=jnp.float32
        ).astype(jnp.bfloat16)
        inner = jnp.einsum("bakl,bcrl->acbkr", far_v, picked, preferred_element_type=jnp.float32)
        coef_real = jnp.where(kept, inner[0, 0] - inner[1, 1], 0.0)
        coef_imag = jnp.where(kept, inner[0, 1] + inner[1, 0], 0.0)
        coefs = jnp.stack([coef_real, coef_imag], axis=1).astype(jnp.bfloat16)
        arrived = lax.all_to_all(into_slots(coefs), "row", split_axis=0, concat_axis=0, tiled=True)
        arrived = arrived.reshape(slots_count, 2, rank_size, rhs_dev)
        rotated = jnp.stack([-arrived[:, 1], arrived[:, 0]], axis=1)
        mixed = jnp.stack([arrived, rotated], axis=1)
        weighted = spread[:, :, None, None, None, None] * mixed[None]
        far_term = jnp.einsum(
            "msaokr,sakl->orml", weighted, received_u, preferred_element_type=jnp.float32
        )
        current = (near_term + far_term).reshape(2, rhs_dev, panels_dev)
    return current


def solution(mesh):
    return jax.shard_map(
        on_device,
        mesh=mesh,
        in_specs=(
            P(None, "rhs", "row"),
            P("row", None, None, None, None),
            P("row", None),
            P("row", None, None, None),
            P("row", None, None, "rhs"),
            P("row"),
            P("row"),
            P("row", None),
            P("row"),
        ),
        out_specs=P(None, "rhs", "row"),
        check_vma=False,
    )
```

profile of v0, /device:TPU:32, one launch (start us, length us, event | category | flops | bytes accessed | tf_op | source)
XLA Modules:
  0.0 553.4 jit_solution(13671830333185340818)
XLA Ops:
  10.5 15.0 %all-to-all-start.1 = ((s32[128,1,2]{2,1,0:T(1,128)}), s32[128,1,2]{2,1,0:T(1,128)S(1)}, u32[]{:S(2)}, u32[]{:S(2)}) async-start(s32[128,1,2]{2,1,0:T(1,128)} %bitcast.14), calls=%async_computation.1 | async-start | bytes 131072 | tf_op jit(solution)/shard_map/all_to_all | solution.py:60
  28.3 6.1 %fusion.24 = f32[128,2,24,2,24]{4,2,3,1,0:T(8,128)} fusion(bf16[128,2,24,256]{3,2,1,0:T(8,128)(2,1)S(1)} %copy-done, bf16[128,2,24,256,1]{3,0,2,1,4:T(8,128)(2,1)S(1)} %convert_bitcast_fusion.3), kind=kOutput, calls=%fused_computation.25 | convolution fusion | flops 150994944 | bytes 7471104 | tf_op jit(solution)/shard_map/bakl,bcrl->acbkr/dot_general | solution.py:92
  34.4 6.3 %copy.201 = f32[128,2,24,2,24]{0,2,4,1,3:T(8,128)} copy(f32[128,2,24,2,24]{4,2,3,1,0:T(8,128)} %fusion.24) | data formatting | bytes 2359296 | tf_op jit(solution)/shard_map/bakl,bcrl->acbkr/dot_general | solution.py:92
  43.3 6.2 %reshape.453 = bf16[128,2,2,24,24]{4,3,2,1,0:T(8,128)(2,1)} reshape(bf16[256,1152]{1,0:T(8,128)(2,1)} %convolution_convert_fusion.4) | data formatting | bytes 1179648 | tf_op jit(solution)/shard_map/reshape | solution.py:55
  49.4 6.4 %reshape.506 = bf16[128,2,1152]{2,1,0:T(2,128)(2,1)} reshape(bf16[128,2,2,24,24]{4,3,2,1,0:T(8,128)(2,1)} %reshape.453) | data formatting | bytes 1179648
  55.8 14.1 %all-to-all-start.2 = ((bf16[128,2,1152]{2,1,0:T(2,128)(2,1)}), bf16[128,2,1152]{2,1,0:T(2,128)(2,1)}, u32[]{:S(2)}, u32[]{:S(2)}) async-start(bf16[128,2,1152]{2,1,0:T(2,128)(2,1)} %reshape.506), calls=%async_computation.2 | async-start | bytes 1179648 | tf_op jit(solution)/shard_map/all_to_all | solution.py:96
  69.9 3.2 copy.312
  74.9 4.6 copy.313
  79.6 11.2 %all-to-all-done.2 = bf16[128,2,1152]{2,1,0:T(2,128)(2,1)} async-done(((bf16[128,2,1152]{2,1,0:T(2,128)(2,1)}), bf16[128,2,1152]{2,1,0:T(2,128)(2,1)}, u32[]{:S(2)}, u32[]{:S(2)}) %all-to-all-start.2) | async-done | bytes 589856 | tf_op jit(solution)/shard_map/all_to_all | solution.py:96
  90.8 7.8 %all-to-all-start = ((bf16[128,2,2,24,256]{4,3,2,1,0:T(8,128)(2,1)}), bf16[128,2,2,24,256]{4,3,2,1,0:T(8,128)(2,1)}, u32[]{:S(2)}, u32[]{:S(2)}) async-start(bf16[128,2,2,24,256]{4,3,2,1,0:T(8,128)(2,1)} %bitcast.337), calls=%async_computation | async-start | bytes 12582912 | tf_op jit(solution)/shard_map/all_to_all | solution.py:59
  99.2 3.4 collective-permute-start
  102.6 6.7 %collective-permute-start.1 = (bf16[2,24,512]{2,1,0:T(8,128)(2,1)}, bf16[2,24,512]{2,1,0:T(8,128)(2,1)S(1)}, u32[]{:S(2)}, u32[]{:S(2)}) collective-permute-start(bf16[2,24,512]{2,1,0:T(8,128)(2,1)} %get-tuple-element.28), channel_id=1, source_target_pairs={{2,0},{4,2},{6,4},{8,6},{10,8},{12,10},{14,12},{16,14},{18,16},{20... | collective-permute-start | bytes 147464 | tf_op jit(solution)/shard_map/ppermute | solution.py:17
  111.4 124.0 %collective-permute-done = bf16[2,24,512]{2,1,0:T(8,128)(2,1)S(1)} collective-permute-done((bf16[2,24,512]{2,1,0:T(8,128)(2,1)}, bf16[2,24,512]{2,1,0:T(8,128)(2,1)S(1)}, u32[]{:S(2)}, u32[]{:S(2)}) %collective-permute-start) | collective-permute-done | bytes 49184 | tf_op jit(solution)/shard_map/ppermute | solution.py:14
  235.7 3.5 fusion.48
  239.9 6.9 %reshape.507 = bf16[128,2,2,24,24]{4,3,2,1,0:T(8,128)(2,1)} reshape(bf16[128,2,1152]{2,1,0:T(2,128)(2,1)} %all-to-all-done.2) | data formatting | bytes 1179648
  246.9 4.1 fusion.183
  251.0 1.9 copy.293
  253.7 1.9 copy.294
  255.6 4.8 copy.204
  262.3 7.5 %fusion.105 = bf16[2,24,4,256]{3,1,2,0:T(8,128)(2,1)S(1)} fusion(bf16[4,256]{1,0:T(4,128)(2,1)} %fusion.170, bf16[256,2,24,256]{3,2,1,0:T(8,128)(2,1)} %bitcast.12, f32[1,24,4,256]{3,1,2,0:T(8,128)S(1)} %fusion.157, f32[1,24,4,256]{3,1,2,0:T(8,128)} %fusion.159, bf16[256,1,2,24,24]{0,4,3,2,1:T(8,128)(2,1)} %maximum_bitcast_fusion, ...), kind=kOutput, calls=%fused_computation.78 | convolution fusion | flops 1218134016 | bytes 7768064 | tf_op jit(solution)/shard_map/msaokr,sakl->orml/dot_general | solution.py:101
  270.8 6.1 %fusion.22 = f32[128,2,24,2,24]{4,2,3,1,0:T(8,128)} fusion(bf16[128,2,24,256]{3,2,1,0:T(8,128)(2,1)S(1)} %copy-done, bf16[128,2,24,256,1]{3,0,2,1,4:T(8,128)(2,1)S(1)} %convert_bitcast_fusion.2), kind=kOutput, calls=%fused_computation.23 | convolution fusion | flops 150994944 | bytes 7471104 | tf_op jit(solution)/shard_map/bakl,bcrl->acbkr/dot_general | solution.py:92
  276.9 6.6 %copy.213 = f32[128,2,24,2,24]{0,2,4,1,3:T(8,128)} copy(f32[128,2,24,2,24]{4,2,3,1,0:T(8,128)} %fusion.22) | data formatting | bytes 2359296 | tf_op jit(solution)/shard_map/bakl,bcrl->acbkr/dot_general | solution.py:92
  286.7 8.1 %collective-permute-start.3 = (bf16[2,24,512]{2,1,0:T(8,128)(2,1)S(1)}, bf16[2,24,512]{2,1,0:T(8,128)(2,1)S(1)}, u32[]{:S(2)}, u32[]{:S(2)}) collective-permute-start(bf16[2,24,512]{2,1,0:T(8,128)(2,1)S(1)} %get-tuple-element.26), channel_id=1, source_target_pairs={{2,0},{4,2},{6,4},{8,6},{10,8},{12,10},{14,12},{16,14},{18,16},{20... | collective-permute-start | bytes 147464 | tf_op jit(solution)/shard_map/ppermute | solution.py:17
  296.0 6.2 %reshape.456 = bf16[128,2,2,24,24]{4,3,2,1,0:T(8,128)(2,1)} reshape(bf16[256,1152]{1,0:T(8,128)(2,1)} %convolution_convert_fusion.3) | data formatting | bytes 1179648 | tf_op jit(solution)/shard_map/reshape | solution.py:55
  302.2 6.4 %reshape.508 = bf16[128,2,1152]{2,1,0:T(2,128)(2,1)} reshape(bf16[128,2,2,24,24]{4,3,2,1,0:T(8,128)(2,1)} %reshape.456) | data formatting | bytes 1179648
  308.6 10.8 %all-to-all-start.3 = ((bf16[128,2,1152]{2,1,0:T(2,128)(2,1)}), bf16[128,2,1152]{2,1,0:T(2,128)(2,1)}, u32[]{:S(2)}, u32[]{:S(2)}) async-start(bf16[128,2,1152]{2,1,0:T(2,128)(2,1)} %reshape.508), calls=%async_computation.3 | async-start | bytes 1179648 | tf_op jit(solution)/shard_map/all_to_all | solution.py:96
  319.8 3.5 fusion.51
  324.0 13.6 %all-to-all-done.3 = bf16[128,2,1152]{2,1,0:T(2,128)(2,1)} async-done(((bf16[128,2,1152]{2,1,0:T(2,128)(2,1)}), bf16[128,2,1152]{2,1,0:T(2,128)(2,1)}, u32[]{:S(2)}, u32[]{:S(2)}) %all-to-all-start.3) | async-done | bytes 589856 | tf_op jit(solution)/shard_map/all_to_all | solution.py:96
  337.6 6.8 %reshape.509 = bf16[128,2,2,24,24]{4,3,2,1,0:T(8,128)(2,1)} reshape(bf16[128,2,1152]{2,1,0:T(2,128)(2,1)} %all-to-all-done.3) | data formatting | bytes 1179648
  344.3 4.1 fusion.182
  348.4 1.9 copy.297
  351.1 1.9 copy.298
  353.1 5.1 copy.216
  359.2 7.2 %fusion.110 = bf16[2,24,4,256]{3,1,2,0:T(8,128)(2,1)S(1)} fusion(bf16[4,256]{1,0:T(4,128)(2,1)} %fusion.170, bf16[256,2,24,256]{3,2,1,0:T(8,128)(2,1)} %bitcast.12, f32[1,24,4,256]{3,1,2,0:T(8,128)S(1)} %fusion.154, f32[1,24,4,256]{3,1,2,0:T(8,128)} %fusion.156, bf16[256,1,2,24,24]{0,4,3,2,1:T(8,128)(2,1)S(1)} %maximum_bitcast_fusion.1, ...), kind=kOutput, calls=%fused_computation.79 | convolution fusion | flops 1218134016 | bytes 7768064 | tf_op jit(solution)/shard_map/msaokr,sakl->orml/dot_general | solution.py:101
  367.5 6.1 %fusion.18 = f32[128,2,24,2,24]{4,2,3,1,0:T(8,128)} fusion(bf16[128,2,24,256,1]{3,0,2,1,4:T(8,128)(2,1)S(1)} %convert_bitcast_fusion.1, bf16[128,2,24,256]{3,2,1,0:T(8,128)(2,1)S(1)} %copy-done), kind=kOutput, calls=%fused_computation.19 | convolution fusion | flops 150994944 | bytes 7471104 | tf_op jit(solution)/shard_map/bakl,bcrl->acbkr/dot_general | solution.py:92
  373.6 6.4 %copy.225 = f32[128,2,24,2,24]{0,2,4,1,3:T(8,128)} copy(f32[128,2,24,2,24]{4,2,3,1,0:T(8,128)} %fusion.18) | data formatting | bytes 2359296 | tf_op jit(solution)/shard_map/bakl,bcrl->acbkr/dot_general | solution.py:92
  381.3 2.5 collective-permute-start.4
  383.8 7.6 %collective-permute-start.5 = (bf16[2,24,512]{2,1,0:T(8,128)(2,1)S(1)}, bf16[2,24,512]{2,1,0:T(8,128)(2,1)S(1)}, u32[]{:S(2)}, u32[]{:S(2)}) collective-permute-start(bf16[2,24,512]{2,1,0:T(8,128)(2,1)S(1)} %get-tuple-element.24), channel_id=1, source_target_pairs={{2,0},{4,2},{6,4},{8,6},{10,8},{12,10},{14,12},{16,14},{18,16},{20... | collective-permute-start | bytes 147464 | tf_op jit(solution)/shard_map/ppermute | solution.py:17
  392.5 6.3 %reshape.459 = bf16[128,2,2,24,24]{4,3,2,1,0:T(8,128)(2,1)} reshape(bf16[256,1152]{1,0:T(8,128)(2,1)} %convolution_convert_fusion.2) | data formatting | bytes 1179648 | tf_op jit(solution)/shard_map/reshape | solution.py:55
  398.9 6.4 %reshape.510 = bf16[128,2,1152]{2,1,0:T(2,128)(2,1)} reshape(bf16[128,2,2,24,24]{4,3,2,1,0:T(8,128)(2,1)} %reshape.459) | data formatting | bytes 1179648
  405.2 6.4 %all-to-all-start.4 = ((bf16[128,2,1152]{2,1,0:T(2,128)(2,1)}), bf16[128,2,1152]{2,1,0:T(2,128)(2,1)}, u32[]{:S(2)}, u32[]{:S(2)}) async-start(bf16[128,2,1152]{2,1,0:T(2,128)(2,1)} %reshape.510), calls=%async_computation.4 | async-start | bytes 1179648 | tf_op jit(solution)/shard_map/all_to_all | solution.py:96
  412.0 3.5 fusion.54
  416.2 10.2 %all-to-all-done.4 = bf16[128,2,1152]{2,1,0:T(2,128)(2,1)} async-done(((bf16[128,2,1152]{2,1,0:T(2,128)(2,1)}), bf16[128,2,1152]{2,1,0:T(2,128)(2,1)}, u32[]{:S(2)}, u32[]{:S(2)}) %all-to-all-start.4) | async-done | bytes 589856 | tf_op jit(solution)/shard_map/all_to_all | solution.py:96
  426.4 6.8 %reshape.511 = bf16[128,2,2,24,24]{4,3,2,1,0:T(8,128)(2,1)} reshape(bf16[128,2,1152]{2,1,0:T(2,128)(2,1)} %all-to-all-done.4) | data formatting | bytes 1179648
  433.2 4.1 fusion.181
  437.3 1.9 copy.301
  439.9 1.9 copy.302
  441.9 4.9 copy.228
  447.8 7.2 %fusion.115 = bf16[2,24,4,256]{3,1,2,0:T(8,128)(2,1)S(1)} fusion(bf16[4,256]{1,0:T(4,128)(2,1)} %fusion.170, bf16[256,2,24,256]{3,2,1,0:T(8,128)(2,1)} %bitcast.12, f32[1,24,4,256]{3,1,2,0:T(8,128)S(1)} %fusion.151, f32[1,24,4,256]{3,1,2,0:T(8,128)} %fusion.153, bf16[256,1,2,24,24]{0,4,3,2,1:T(8,128)(2,1)S(1)} %maximum_bitcast_fusion.2, ...), kind=kOutput, calls=%fused_computation.80 | convolution fusion | flops 1218134016 | bytes 7768064 | tf_op jit(solution)/shard_map/msaokr,sakl->orml/dot_general | solution.py:101
  456.1 6.1 %fusion.16 = f32[128,2,24,2,24]{4,2,3,1,0:T(8,128)} fusion(bf16[128,2,24,256,1]{3,0,2,1,4:T(8,128)(2,1)S(1)} %convert_bitcast_fusion, bf16[128,2,24,256]{3,2,1,0:T(8,128)(2,1)S(1)} %copy-done), kind=kOutput, calls=%fused_computation.17 | convolution fusion | flops 150994944 | bytes 7471104 | tf_op jit(solution)/shard_map/bakl,bcrl->acbkr/dot_general | solution.py:92
  462.2 6.4 %copy.237 = f32[128,2,24,2,24]{0,2,4,1,3:T(8,128)} copy(f32[128,2,24,2,24]{4,2,3,1,0:T(8,128)} %fusion.16) | data formatting | bytes 2359296 | tf_op jit(solution)/shard_map/bakl,bcrl->acbkr/dot_general | solution.py:92
  469.9 2.4 collective-permute-start.6
  472.3 7.7 %collective-permute-start.7 = (bf16[2,24,512]{2,1,0:T(8,128)(2,1)S(1)}, bf16[2,24,512]{2,1,0:T(8,128)(2,1)S(1)}, u32[]{:S(2)}, u32[]{:S(2)}) collective-permute-start(bf16[2,24,512]{2,1,0:T(8,128)(2,1)S(1)} %get-tuple-element.22), channel_id=1, source_target_pairs={{2,0},{4,2},{6,4},{8,6},{10,8},{12,10},{14,12},{16,14},{18,16},{20... | collective-permute-start | bytes 147464 | tf_op jit(solution)/shard_map/ppermute | solution.py:17
  481.2 6.4 %reshape.462 = bf16[128,2,2,24,24]{4,3,2,1,0:T(8,128)(2,1)} reshape(bf16[256,1152]{1,0:T(8,128)(2,1)} %convolution_convert_fusion.1) | data formatting | bytes 1179648 | tf_op jit(solution)/shard_map/reshape | solution.py:55
  487.6 6.4 %reshape.512 = bf16[128,2,1152]{2,1,0:T(2,128)(2,1)} reshape(bf16[128,2,2,24,24]{4,3,2,1,0:T(8,128)(2,1)} %reshape.462) | data formatting | bytes 1179648
  493.9 6.4 %all-to-all-start.5 = ((bf16[128,2,1152]{2,1,0:T(2,128)(2,1)}), bf16[128,2,1152]{2,1,0:T(2,128)(2,1)}, u32[]{:S(2)}, u32[]{:S(2)}) async-start(bf16[128,2,1152]{2,1,0:T(2,128)(2,1)} %reshape.512), calls=%async_computation.5 | async-start | bytes 1179648 | tf_op jit(solution)/shard_map/all_to_all | solution.py:96
  500.7 3.5 fusion.57
  504.9 11.9 %all-to-all-done.5 = bf16[128,2,1152]{2,1,0:T(2,128)(2,1)} async-done(((bf16[128,2,1152]{2,1,0:T(2,128)(2,1)}), bf16[128,2,1152]{2,1,0:T(2,128)(2,1)}, u32[]{:S(2)}, u32[]{:S(2)}) %all-to-all-start.5) | async-done | bytes 589856 | tf_op jit(solution)/shard_map/all_to_all | solution.py:96
  516.8 6.8 %reshape.513 = bf16[128,2,2,24,24]{4,3,2,1,0:T(8,128)(2,1)} reshape(bf16[128,2,1152]{2,1,0:T(2,128)(2,1)} %all-to-all-done.5) | data formatting | bytes 1179648
  523.6 4.1 fusion.180
  527.7 1.9 copy.305
  530.4 1.9 copy.306
  532.3 4.7 copy.240
  538.1 7.4 %fusion.85 = f32[2,4,3,8,256]{4,3,2,1,0:T(8,128)S(1)} fusion(bf16[4,256]{1,0:T(4,128)(2,1)S(1)} %copy-done.2, bf16[256,2,24,256]{3,2,1,0:T(8,128)(2,1)} %bitcast.12, f32[1,24,4,256]{3,1,2,0:T(8,128)S(1)} %fusion.148, f32[1,24,4,256]{3,1,2,0:T(8,128)} %fusion.150, bf16[256,1,2,24,24]{0,4,3,2,1:T(8,128)(2,1)S(1)} %maximum_bitcast_fusion.3, ...), kind=kOutput, calls=%fused_computation.74 | convolution fusion | flops 1218084864 | bytes 7866368 | tf_op jit(solution)/shard_map/msaokr,sakl->orml/dot_general | solution.py:101
  (88 shorter events, 39.1 us)
Async XLA Ops:
  6.5 21.8 %copy-start = (bf16[128,2,24,256]{3,2,1,0:T(8,128)(2,1)S(1)}, bf16[128,2,24,256]{3,2,1,0:T(8,128)(2,1)}, u32[]{:S(2)}) copy-start(bf16[128,2,24,256]{3,2,1,0:T(8,128)(2,1)} %param.12) | copy-start | bytes 9437188
  6.5 63.4 %all-gather.2.cloned.1.call-start = ((), (), s32[]{:S(2)}) async-start(), calls=%async_computation.6 | async-start | bytes 4718592 | tf_op jit(solution)/shard_map/all_gather | solution.py:57
  10.5 45.2 %all-to-all-start.1 = ((s32[128,1,2]{2,1,0:T(1,128)}), s32[128,1,2]{2,1,0:T(1,128)S(1)}, u32[]{:S(2)}, u32[]{:S(2)}) async-start(s32[128,1,2]{2,1,0:T(1,128)} %bitcast.14), calls=%async_computation.1 | async-start | bytes 131072 | tf_op jit(solution)/shard_map/all_to_all | solution.py:60
  34.4 6.3 %copy-start.4 = (s32[128]{0:T(128)S(1)}, s32[128]{0:T(128)}, u32[]{:S(2)}) copy-start(s32[128]{0:T(128)} %param.14) | copy-start | bytes 1540
  55.8 35.0 %all-to-all-start.2 = ((bf16[128,2,1152]{2,1,0:T(2,128)(2,1)}), bf16[128,2,1152]{2,1,0:T(2,128)(2,1)}, u32[]{:S(2)}, u32[]{:S(2)}) async-start(bf16[128,2,1152]{2,1,0:T(2,128)(2,1)} %reshape.506), calls=%async_computation.2 | async-start | bytes 1179648 | tf_op jit(solution)/shard_map/all_to_all | solution.py:96
  90.8 18.5 %copy-start.3 = (s32[4,4]{1,0:T(4,128)S(1)}, s32[4,4]{1,0:T(4,128)}, u32[]{:S(2)}) copy-start(s32[4,4]{1,0:T(4,128)} %param.11) | copy-start | bytes 196
  90.8 171.5 %all-to-all-start = ((bf16[128,2,2,24,256]{4,3,2,1,0:T(8,128)(2,1)}), bf16[128,2,2,24,256]{4,3,2,1,0:T(8,128)(2,1)}, u32[]{:S(2)}, u32[]{:S(2)}) async-start(bf16[128,2,2,24,256]{4,3,2,1,0:T(8,128)(2,1)} %bitcast.337), calls=%async_computation | async-start | bytes 12582912 | tf_op jit(solution)/shard_map/all_to_all | solution.py:59
  99.2 136.1 %collective-permute-start = (bf16[2,24,512]{2,1,0:T(8,128)(2,1)}, bf16[2,24,512]{2,1,0:T(8,128)(2,1)S(1)}, u32[]{:S(2)}, u32[]{:S(2)}) collective-permute-start(bf16[2,24,512]{2,1,0:T(8,128)(2,1)} %get-tuple-element.27), channel_id=1, source_target_pairs={{0,2},{2,4},{4,6},{6,8},{8,10},{10,12},{12,14},{14,16},{16,18},{18... | collective-permute-start | bytes 147464 | tf_op jit(solution)/shard_map/ppermute | solution.py:14
  102.6 132.8 %collective-permute-start.1 = (bf16[2,24,512]{2,1,0:T(8,128)(2,1)}, bf16[2,24,512]{2,1,0:T(8,128)(2,1)S(1)}, u32[]{:S(2)}, u32[]{:S(2)}) collective-permute-start(bf16[2,24,512]{2,1,0:T(8,128)(2,1)} %get-tuple-element.28), channel_id=1, source_target_pairs={{2,0},{4,2},{6,4},{8,6},{10,8},{12,10},{14,12},{16,14},{18,16},{20... | collective-permute-start | bytes 147464 | tf_op jit(solution)/shard_map/ppermute | solution.py:17
  262.3 7.5 %copy-start.1 = (s32[128]{0:T(128)S(1)}, s32[128]{0:T(128)}, u32[]{:S(2)}) copy-start(s32[128]{0:T(128)} %param.15) | copy-start | bytes 1540
  284.8 34.6 %collective-permute-start.2 = (bf16[2,24,512]{2,1,0:T(8,128)(2,1)S(1)}, bf16[2,24,512]{2,1,0:T(8,128)(2,1)S(1)}, u32[]{:S(2)}, u32[]{:S(2)}) collective-permute-start(bf16[2,24,512]{2,1,0:T(8,128)(2,1)S(1)} %get-tuple-element.25), channel_id=1, source_target_pairs={{0,2},{2,4},{4,6},{6,8},{8,10},{10,12},{12,14},{14,16},{16,18},{18... | collective-permute-start | bytes 147464 | tf_op jit(solution)/shard_map/ppermute | solution.py:14
  286.7 32.7 %collective-permute-start.3 = (bf16[2,24,512]{2,1,0:T(8,128)(2,1)S(1)}, bf16[2,24,512]{2,1,0:T(8,128)(2,1)S(1)}, u32[]{:S(2)}, u32[]{:S(2)}) collective-permute-start(bf16[2,24,512]{2,1,0:T(8,128)(2,1)S(1)} %get-tuple-element.26), channel_id=1, source_target_pairs={{2,0},{4,2},{6,4},{8,6},{10,8},{12,10},{14,12},{16,14},{18,16},{20... | collective-permute-start | bytes 147464 | tf_op jit(solution)/shard_map/ppermute | solution.py:17
  308.6 29.0 %all-to-all-start.3 = ((bf16[128,2,1152]{2,1,0:T(2,128)(2,1)}), bf16[128,2,1152]{2,1,0:T(2,128)(2,1)}, u32[]{:S(2)}, u32[]{:S(2)}) async-start(bf16[128,2,1152]{2,1,0:T(2,128)(2,1)} %reshape.508), calls=%async_computation.3 | async-start | bytes 1179648 | tf_op jit(solution)/shard_map/all_to_all | solution.py:96
  381.3 30.3 %collective-permute-start.4 = (bf16[2,24,512]{2,1,0:T(8,128)(2,1)S(1)}, bf16[2,24,512]{2,1,0:T(8,128)(2,1)S(1)}, u32[]{:S(2)}, u32[]{:S(2)}) collective-permute-start(bf16[2,24,512]{2,1,0:T(8,128)(2,1)S(1)} %get-tuple-element.23), channel_id=1, source_target_pairs={{0,2},{2,4},{4,6},{6,8},{8,10},{10,12},{12,14},{14,16},{16,18},{18... | collective-permute-start | bytes 147464 | tf_op jit(solution)/shard_map/ppermute | solution.py:14
  383.8 27.8 %collective-permute-start.5 = (bf16[2,24,512]{2,1,0:T(8,128)(2,1)S(1)}, bf16[2,24,512]{2,1,0:T(8,128)(2,1)S(1)}, u32[]{:S(2)}, u32[]{:S(2)}) collective-permute-start(bf16[2,24,512]{2,1,0:T(8,128)(2,1)S(1)} %get-tuple-element.24), channel_id=1, source_target_pairs={{2,0},{4,2},{6,4},{8,6},{10,8},{12,10},{14,12},{16,14},{18,16},{20... | collective-permute-start | bytes 147464 | tf_op jit(solution)/shard_map/ppermute | solution.py:17
  405.2 21.2 %all-to-all-start.4 = ((bf16[128,2,1152]{2,1,0:T(2,128)(2,1)}), bf16[128,2,1152]{2,1,0:T(2,128)(2,1)}, u32[]{:S(2)}, u32[]{:S(2)}) async-start(bf16[128,2,1152]{2,1,0:T(2,128)(2,1)} %reshape.510), calls=%async_computation.4 | async-start | bytes 1179648 | tf_op jit(solution)/shard_map/all_to_all | solution.py:96
  469.9 30.4 %collective-permute-start.6 = (bf16[2,24,512]{2,1,0:T(8,128)(2,1)S(1)}, bf16[2,24,512]{2,1,0:T(8,128)(2,1)S(1)}, u32[]{:S(2)}, u32[]{:S(2)}) collective-permute-start(bf16[2,24,512]{2,1,0:T(8,128)(2,1)S(1)} %get-tuple-element.21), channel_id=1, source_target_pairs={{0,2},{2,4},{4,6},{6,8},{8,10},{10,12},{12,14},{14,16},{16,18},{18... | collective-permute-start | bytes 147464 | tf_op jit(solution)/shard_map/ppermute | solution.py:14
  472.3 28.0 %collective-permute-start.7 = (bf16[2,24,512]{2,1,0:T(8,128)(2,1)S(1)}, bf16[2,24,512]{2,1,0:T(8,128)(2,1)S(1)}, u32[]{:S(2)}, u32[]{:S(2)}) collective-permute-start(bf16[2,24,512]{2,1,0:T(8,128)(2,1)S(1)} %get-tuple-element.22), channel_id=1, source_target_pairs={{2,0},{4,2},{6,4},{8,6},{10,8},{12,10},{14,12},{16,14},{18,16},{20... | collective-permute-start | bytes 147464 | tf_op jit(solution)/shard_map/ppermute | solution.py:17
  493.9 22.9 %all-to-all-start.5 = ((bf16[128,2,1152]{2,1,0:T(2,128)(2,1)}), bf16[128,2,1152]{2,1,0:T(2,128)(2,1)}, u32[]{:S(2)}, u32[]{:S(2)}) async-start(bf16[128,2,1152]{2,1,0:T(2,128)(2,1)} %reshape.512), calls=%async_computation.5 | async-start | bytes 1179648 | tf_op jit(solution)/shard_map/all_to_all | solution.py:96
  530.4 7.7 %copy-start.2 = (bf16[4,256]{1,0:T(4,128)(2,1)S(1)}, bf16[4,256]{1,0:T(4,128)(2,1)}, u32[]{:S(2)}) copy-start(bf16[4,256]{1,0:T(4,128)(2,1)} %fusion.170) | copy-start | bytes 6148
Sparse Core Ops, SparseCore 0:
  9.1 19.6 all-gather.1
where the time goes:
time: 564 us; the launch traced here: 553 us
  waiting for transfers between devices  172 us (30%)
  local copies, waits for them, and re-layouts  166 us (29%)
  starting transfers between devices  101 us (18%)
  matrix products  80 us (14%)
  other arithmetic  20.9 us (4%)
  between operations  14.5 us (3%)
    ppermute x4, waiting for transfers between devices, padded_2(): lax.ppermute(lax.slice_in_dim(block, block.shape[dim] - width, None, axis...  124 us
    unnamed x32, local copies, waits for them, and re-layouts  76.1 us
    all_to_all x4, waiting for transfers between devices, on_device(): lax.all_to_all(into_slots(coefs), 'row', split_axis=0, concat_axis=0, til...  46.9 us
    all_to_all x4, starting transfers between devices, on_device(): lax.all_to_all(into_slots(coefs), 'row', split_axis=0, concat_axis=0, til...  37.7 us
    ppermute x4, starting transfers between devices, padded_2(): lax.ppermute(lax.slice_in_dim(block, 0, width, axis=dim), axis, backward)  30.1 us
    dot_general x4, matrix products, on_device(): jnp.einsum('msaokr,sakl->orml', weighted, received_u, preferred_element_t...  29.3 us
    dot_general x4, local copies, waits for them, and re-layouts, on_device(): jnp.einsum('bakl,bcrl->acbkr', far_v, picked, preferred_element_type=jnp....  25.7 us
    reshape x4, local copies, waits for them, and re-layouts, into_slots(): return placed.reshape((rows_count, capacity) + values.shape[1:])  25.1 us
  transfers between devices with their start and end apart: 15, of which 5 were waited for; matrix products, arithmetic and copies ran while one was open for 23% of the time, Pallas kernels for 0%

commit v1 on v0

v1 whole, which is shorter than its diff:
```python
import functools

import jax
import jax.numpy as jnp
from jax import lax
from jax.experimental import pallas as pl
from jax.experimental.pallas import tpu as pltpu
from jax.sharding import PartitionSpec as P

APPS = 4
BF = jnp.bfloat16
F32 = jnp.float32
VMEM_LIMIT = 56 * 1024 * 1024


def dot(a, b):
    return jnp.dot(a, b, preferred_element_type=F32)


def next_slot(count_ref, destination):
    slot = count_ref[destination]
    count_ref[destination] = slot + 1
    return slot


def clear_counts(count_ref, count):
    def body(i, carry):
        count_ref[i] = 0
        return carry

    lax.fori_loop(0, count, body, 0)


def place_u_kernel(dest_ref, u_ref, out_ref, count_ref):
    clear_counts(count_ref, out_ref.shape[0])
    out_ref[...] = jnp.zeros_like(out_ref)
    half = u_ref.shape[3]

    def body(b, carry):
        d = dest_ref[b]
        s = next_slot(count_ref, d)
        for c in range(2):
            lane = pl.multiple_of(s * (2 * half) + c * half, half)
            out_ref[d, :, pl.ds(lane, half)] = u_ref[b, c]
        return carry

    lax.fori_loop(0, u_ref.shape[0], body, 0)


def place_v_kernel(
    dest_ref, rank_ref, col_ref, row_ref, v_ref, out_ref, mask_ref, tag_ref, count_ref
):
    clear_counts(count_ref, out_ref.shape[0])
    out_ref[...] = jnp.zeros_like(out_ref)
    mask_ref[...] = jnp.zeros_like(mask_ref)
    tag_ref[...] = jnp.zeros_like(tag_ref)
    rank_size, leaf = v_ref.shape[2], v_ref.shape[3]
    group = lax.broadcasted_iota(jnp.int32, (rank_size, 256), 1) // 64
    index = lax.broadcasted_iota(jnp.int32, (rank_size, 256), 0)
    lane = lax.broadcasted_iota(jnp.int32, (rank_size, 128), 1)

    def body(b, carry):
        d = dest_ref[b]
        s = next_slot(count_ref, d)
        for c in range(2):
            at = pl.multiple_of(s * (2 * leaf) + c * leaf, leaf)
            out_ref[d, :, pl.ds(at, leaf)] = v_ref[b, c]
        kept = (group == col_ref[b]) & (index < rank_ref[b])
        mask_ref[d, :, pl.ds(pl.multiple_of(s * 256, 256), 256)] = jnp.where(kept, 1.0, 0.0).astype(
            BF
        )
        tag = jnp.where(lane == s * 64 + 48 + row_ref[b], 1.0, 0.0)
        tag_ref[d] = (tag_ref[d].astype(F32) + tag).astype(BF)
        return carry

    lax.fori_loop(0, v_ref.shape[0], body, 0)


def near_kernel(offset_ref, left_ref, low_ref, high_ref, right_ref, a_ref, out_ref, xa_ref, xb_ref):
    i = pl.program_id(0)

    @pl.when(i == 0)
    def _():
        pad = jnp.zeros((16, 256), F32)
        for q, ref in enumerate((left_ref, low_ref, high_ref, right_ref)):
            for j in range(2):
                x = ref[j].astype(F32)
                re, im = x[:24], x[24:]
                xa_ref[q * 2 + j] = jnp.concatenate([re, im, pad], axis=0).T.astype(BF)
                xb_ref[q * 2 + j] = jnp.concatenate([-im, re, pad], axis=0).T.astype(BF)

    total = jnp.zeros((256, 64), F32)
    for k in range(a_ref.shape[1]):
        at = i + offset_ref[i, k] + 2
        total += dot(a_ref[0, k, 0], xa_ref[at]) + dot(a_ref[0, k, 1], xb_ref[at])
    out_ref[...] = total.T[:48]


def stage_kernel(do_u, do_v, steps_u, *refs):
    refs = list(refs)
    core_ref = refs.pop(0)
    i = pl.program_id(0)
    if do_u:
        c_ref, own_ref, other_ref, near_ref = refs[:4]
        refs = refs[4:]
    else:
        field_ref = refs.pop(0)
    if do_v:
        v_ref, mask_ref, tag_ref = refs[:3]
        refs = refs[3:]
        message_ref, low_ref, high_ref = refs[:3]
        refs = refs[3:]
    else:
        out_ref = refs.pop(0)
    if do_u:
        total_ref = refs.pop(0)
    if do_v:
        xw_ref, fold_ref = refs

    def prepare(clusters):
        pad = jnp.zeros((16, 256), F32)
        first, second = [], []
        for m, x in enumerate(clusters):
            rounded = x.astype(BF)
            (low_ref if m < 2 else high_ref)[m % 2] = rounded
            wide = rounded.astype(F32)
            re, im = wide[:24], wide[24:]
            first += [re, im, pad]
            second += [-im, re, pad]
        xw_ref[0] = jnp.concatenate(first, axis=0).T.astype(BF)
        xw_ref[1] = jnp.concatenate(second, axis=0).T.astype(BF)
        row = lax.broadcasted_iota(jnp.int32, (512, 128), 0)
        lane = lax.broadcasted_iota(jnp.int32, (512, 128), 1)
        same = (row // 256 == lane // 64) & (row % 64 == lane % 64)
        fold_ref[...] = jnp.where(same, 1.0, 0.0).astype(BF)

    if do_u:

        @pl.when(i == 0)
        def _():
            total_ref[...] = jnp.zeros_like(total_ref)

        @pl.when(i < steps_u)
        def _():
            turned = c_ref[...].astype(F32).T
            for s in range(2):
                base = turned[s * 64 : s * 64 + 48]
                weights = jnp.concatenate(
                    [
                        (base * turned[s * 64 + 48 + o : s * 64 + 49 + o]).astype(BF)
                        for o in range(4)
                    ],
                    axis=0,
                )
                lanes = slice(s * 256, s * 256 + 256)
                total_ref[0] += dot(weights, own_ref[:, lanes])
                total_ref[1] += dot(weights, other_ref[:, lanes])

        @pl.when(i == steps_u - 1)
        def _():
            first_core = core_ref[0] == 0
            clusters = []
            for o in range(4):
                halves = []
                for w in range(2):
                    z = total_ref[w, o * 48 : o * 48 + 48]
                    re = z[:24, :128] - z[24:, 128:]
                    im = z[24:, :128] + z[:24, 128:]
                    halves.append(jnp.concatenate([re, im], axis=0))
                x = jnp.concatenate(
                    [
                        jnp.where(first_core, halves[0], halves[1]),
                        jnp.where(first_core, halves[1], halves[0]),
                    ],
                    axis=1,
                )
                clusters.append(x + near_ref[:, o * 256 : o * 256 + 256])
            if do_v:
                prepare(clusters)
            else:
                for o in range(4):
                    out_ref[:, o * 256 : o * 256 + 256] = clusters[o]
    else:

        @pl.when(i == 0)
        def _():
            prepare([field_ref[:, m * 256 : m * 256 + 256] for m in range(4)])

    if do_v:

        @pl.when(i >= steps_u)
        def _():
            picked = []
            for s in range(2):
                base = s * 512
                p = dot(v_ref[:, base : base + 256], xw_ref[0])
                p += dot(v_ref[:, base + 256 : base + 512], xw_ref[1])
                picked.append(p.astype(BF) * mask_ref[:, s * 256 : s * 256 + 256])
            folded = dot(jnp.concatenate(picked, axis=1), fold_ref[...])
            message_ref[...] = (folded + tag_ref[...].astype(F32)).astype(BF)


def stage(do_u, do_v, core, *operands):
    steps = 4
    steps_u = steps if do_u else 0
    total_rows = operands[0].shape[0] if do_u else operands[1].shape[0]
    rows = total_rows // steps
    grid = steps_u + (steps if do_v else 0)

    def in_u(i, core_ref):
        return (jnp.minimum(i, steps - 1), 0)

    def in_v(i, core_ref):
        return (jnp.maximum(i - steps_u, 0), 0)

    def whole(rank):
        return lambda i, core_ref: (0,) * rank

    in_specs, scratch = [], []
    if do_u:
        in_specs += [
            pl.BlockSpec((rows, 128), in_u),
            pl.BlockSpec((rows, 512), in_u),
            pl.BlockSpec((rows, 512), in_u),
            pl.BlockSpec((48, 1024), whole(2)),
        ]
        scratch.append(pltpu.VMEM((2, 192, 256), F32))
    else:
        in_specs.append(pl.BlockSpec((48, 1024), whole(2)))
    if do_v:
        in_specs += [
            pl.BlockSpec((rows, 1024), in_v),
            pl.BlockSpec((rows, 512), in_v),
            pl.BlockSpec((rows, 128), in_v),
        ]
        out_shape = [
            jax.ShapeDtypeStruct((total_rows, 128), BF),
            jax.ShapeDtypeStruct((2, 48, 256), BF),
            jax.ShapeDtypeStruct((2, 48, 256), BF),
        ]
        out_specs = [
            pl.BlockSpec((rows, 128), in_v),
            pl.BlockSpec((2, 48, 256), whole(3)),
            pl.BlockSpec((2, 48, 256), whole(3)),
        ]
        scratch += [pltpu.VMEM((2, 256, 256), BF), pltpu.VMEM((512, 128), BF)]
    else:
        out_shape = jax.ShapeDtypeStruct((48, 1024), F32)
        out_specs = pl.BlockSpec((48, 1024), whole(2))
    return pl.pallas_call(
        functools.partial(stage_kernel, do_u, do_v, steps_u),
        grid_spec=pltpu.PrefetchScalarGridSpec(
            num_scalar_prefetch=1,
            grid=(grid,),
            in_specs=in_specs,
            out_specs=out_specs,
            scratch_shapes=scratch,
        ),
        out_shape=out_shape,
        compiler_params=pltpu.CompilerParams(vmem_limit_bytes=VMEM_LIMIT),
        cost_estimate=pl.CostEstimate(
            flops=6_000_000_000, bytes_accessed=16_000_000, transcendentals=0
        ),
    )(core, *operands)


def near_call(offsets, left, low, high, right, blocks):
    clusters, near = blocks.shape[:2]
    whole = pl.BlockSpec((2, 48, 256), lambda i, offset_ref: (0, 0, 0))
    return pl.pallas_call(
        near_kernel,
        grid_spec=pltpu.PrefetchScalarGridSpec(
            num_scalar_prefetch=1,
            grid=(clusters,),
            in_specs=[whole] * 4
            + [pl.BlockSpec((1, near, 2, 256, 256), lambda i, offset_ref: (i, 0, 0, 0, 0))],
            out_specs=pl.BlockSpec((48, 256), lambda i, offset_ref: (0, i)),
            scratch_shapes=[pltpu.VMEM((8, 256, 64), BF), pltpu.VMEM((8, 256, 64), BF)],
        ),
        out_shape=jax.ShapeDtypeStruct((48, clusters * 256), F32),
        compiler_params=pltpu.CompilerParams(vmem_limit_bytes=VMEM_LIMIT),
        cost_estimate=pl.CostEstimate(
            flops=3_000_000_000, bytes_accessed=4_500_000, transcendentals=0
        ),
    )(offsets, left, low, high, right, blocks)


def place_u(dest, far_u, count):
    return pl.pallas_call(
        place_u_kernel,
        in_specs=[
            pl.BlockSpec(memory_space=pltpu.SMEM),
            pl.BlockSpec(memory_space=pltpu.VMEM),
        ],
        out_specs=pl.BlockSpec(memory_space=pltpu.VMEM),
        out_shape=jax.ShapeDtypeStruct((count, far_u.shape[2], 4 * far_u.shape[3]), BF),
        scratch_shapes=[pltpu.SMEM((count,), jnp.int32)],
        compiler_params=pltpu.CompilerParams(vmem_limit_bytes=VMEM_LIMIT),
    )(dest, far_u)


def place_v(dest, rank, col, row, far_v, count):
    rank_size, leaf = far_v.shape[2:]
    return pl.pallas_call(
        place_v_kernel,
        in_specs=[pl.BlockSpec(memory_space=pltpu.SMEM)] * 4
        + [pl.BlockSpec(memory_space=pltpu.VMEM)],
        out_specs=[pl.BlockSpec(memory_space=pltpu.VMEM)] * 3,
        out_shape=[
            jax.ShapeDtypeStruct((count, rank_size, 4 * leaf), BF),
            jax.ShapeDtypeStruct((count, rank_size, 512), BF),
            jax.ShapeDtypeStruct((count, rank_size, 128), BF),
        ],
        scratch_shapes=[pltpu.SMEM((count,), jnp.int32)],
        compiler_params=pltpu.CompilerParams(vmem_limit_bytes=VMEM_LIMIT),
        cost_estimate=pl.CostEstimate(
            flops=6_000_000_000, bytes_accessed=16_000_000, transcendentals=0
        ),
    )(dest, rank, col, row, far_v)


def on_device(
    source_field,
    near_blocks,
    near_offsets,
    far_v,
    far_u,
    far_rank,
    far_col_local,
    far_dest,
    far_row_local,
):
    parts, rhs_dev, panels_dev = source_field.shape
    rank_size = far_v.shape[2]
    count = lax.axis_size("row")
    forward = [(i, i + 1) for i in range(count - 1)]
    backward = [(i + 1, i) for i in range(count - 1)]
    core = lax.axis_index("rhs").astype(jnp.int32).reshape(1)
    dest = far_dest.reshape(-1)

    def exchange(x):
        return lax.all_to_all(x, "row", split_axis=0, concat_axis=0, tiled=True)

    u_own = exchange(place_u(dest, far_u, count)).reshape(count * rank_size, -1)
    u_other = lax.ppermute(u_own, "rhs", [(0, 1), (1, 0)])
    v_slots, mask, tag = place_v(dest, far_rank, far_col_local, far_row_local, far_v, count)
    v_slots = v_slots.reshape(count * rank_size, -1)
    mask = mask.reshape(count * rank_size, -1)
    tag = tag.reshape(count * rank_size, -1)
    message, low, high = stage(
        False, True, core, source_field.reshape(parts * rhs_dev, panels_dev), v_slots, mask, tag
    )
    for application in range(APPS):
        left = lax.ppermute(high, "row", forward)
        right = lax.ppermute(low, "row", backward)
        arrived = exchange(message.reshape(count, rank_size, 128)).reshape(-1, 128)
        near_term = near_call(near_offsets, left, low, high, right, near_blocks)
        if application < APPS - 1:
            message, low, high = stage(
                True, True, core, arrived, u_own, u_other, near_term, v_slots, mask, tag
            )
    result = stage(True, False, core, arrived, u_own, u_other, near_term)
    return result.reshape(parts, rhs_dev, panels_dev)


def solution(mesh):
    return jax.shard_map(
        on_device,
        mesh=mesh,
        in_specs=(
            P(None, "rhs", "row"),
            P("row", None, None, None, None),
            P("row", None),
            P("row", None, None, None),
            P("row", None, None, "rhs"),
            P("row"),
            P("row"),
            P("row", None),
            P("row"),
        ),
        out_specs=P(None, "rhs", "row"),
        check_vma=False,
    )
```

time: 564 us -> 305 us (0.54); the launches traced: 553 us -> 303 us
  local copies, waits for them, and re-layouts: 166 us -> 7.67 us
  waiting for transfers between devices: 172 us -> 38.9 us
  blocking collectives: 0 us -> 89.5 us
  Pallas kernels: 0 us -> 88.6 us
  matrix products: 80 us -> 0 us
  starting transfers between devices: 101 us -> 78.1 us
  other arithmetic: 20.9 us -> 0 us
  between operations: 14.5 us -> 0.14 us
    all_to_all x0 -> x1, blocking collectives: none -> 89.5 us  [exchange(): return lax.all_to_all(x, 'row', split_axis=0, concat_axis=0, tiled=True)]
    pallas_call x0 -> x11, Pallas kernels: none -> 88.6 us  [the longest x5 49.5 us: stage(): pl.pallas_call(functools.partial(stage_kernel, do_u, do_v, steps_u), grid...]
    ppermute x8 -> x9, waiting for transfers between devices: 124 us -> 38.9 us  [the longest x4 38.9 us: on_device(): left = lax.ppermute(high, 'row', forward)]
    dot_general x25 -> x0, matrix products: 80 us -> none  [the longest x4 29.3 us: on_device(): jnp.einsum('msaokr,sakl->orml', weighted, received_u, preferred_element_t...]
    unnamed x32 -> x24, local copies, waits for them, and re-layouts: 76.1 us -> 7.67 us
    all_to_all x6 -> x4, waiting for transfers between devices: 46.9 us -> 0.01 us  [exchange(): return lax.all_to_all(x, 'row', split_axis=0, concat_axis=0, tiled=True)]
    reshape x6 -> x0, local copies, waits for them, and re-layouts: 25.8 us -> none  [the longest x4 25.1 us: into_slots(): return placed.reshape((rows_count, capacity) + values.shape[1:])]
    dot_general x4 -> x0, local copies, waits for them, and re-layouts: 25.7 us -> none  [on_device(): jnp.einsum('bakl,bcrl->acbkr', far_v, picked, preferred_element_type=jnp....]
  transfers between devices with their start and end apart: 15 -> 13, of which waited for: 5 -> 4; matrix products, arithmetic and copies ran while one was open for 23% -> 0% of each run, Pallas kernels for 0% -> 14%
where the time goes in v1:
time: 305 us; the launch traced here: 303 us
  blocking collectives  89.5 us (29%)
  Pallas kernels  88.6 us (29%)
  starting transfers between devices  78.1 us (26%)
  waiting for transfers between devices  38.9 us (13%)
  local copies, waits for them, and re-layouts  7.67 us (3%)
    all_to_all x1, blocking collectives, exchange(): return lax.all_to_all(x, 'row', split_axis=0, concat_axis=0, tiled=True)  89.5 us
    pallas_call x5, Pallas kernels, stage(): pl.pallas_call(functools.partial(stage_kernel, do_u, do_v, steps_u), grid...  49.5 us
    ppermute x4, waiting for transfers between devices, on_device(): left = lax.ppermute(high, 'row', forward)  38.9 us
    all_to_all x4, starting transfers between devices, exchange(): return lax.all_to_all(x, 'row', split_axis=0, concat_axis=0, tiled=True)  37.7 us
    ppermute x4, starting transfers between devices, on_device(): right = lax.ppermute(low, 'row', backward)  26.9 us
    pallas_call x4, Pallas kernels, near_call(): pl.pallas_call(near_kernel, grid_spec=pltpu.PrefetchScalarGridSpec(num_sc...  23.1 us
    ppermute x4, starting transfers between devices, on_device(): left = lax.ppermute(high, 'row', forward)  13.5 us
    pallas_call x1, Pallas kernels, place_v(): pl.pallas_call(place_v_kernel, in_specs=[pl.BlockSpec(memory_space=pltpu....  10.4 us
  transfers between devices with their start and end apart: 13, of which 4 were waited for; matrix products, arithmetic and copies ran while one was open for 0% of the time, Pallas kernels for 14%

profile of v1, /device:TPU:32, one launch (start us, length us, event | category | flops | bytes accessed | tf_op | source)
XLA Modules:
  0.0 302.9 jit_solution(118166998509960433)
XLA Ops:
  0.0 5.7 %shard_map.93 = bf16[128,24,512]{2,1,0:T(8,128)(2,1)} custom-call(s32[128]{0:T(128)} %bitcast.28, bf16[128,2,24,128]{3,2,1,0:T(8,128)(2,1)} %u_ref.1), custom_call_target="tpu_custom_call" | custom-call | tf_op jit(solution)/shard_map/pallas_call | solution.py:289
  5.7 89.5 %all_to_all.25 = bf16[128,24,512]{2,1,0:T(8,128)(2,1)S(1)} all-to-all(bf16[128,24,512]{2,1,0:T(8,128)(2,1)} %shard_map.93), channel_id=1, replica_groups=mesh['row'=128,'rhs'=2] {'row'}, dimensions={0} | all-to-all | bytes 6291456 | tf_op jit(solution)/shard_map/all_to_all | solution.py:342
  95.1 0.0 copy-start
  95.1 0.0 collective-permute-start
  95.1 10.4 %shard_map.91 = (bf16[128,24,1024]{2,1,0:T(8,128)(2,1)}, bf16[128,24,512]{2,1,0:T(8,128)(2,1)}, bf16[128,24,128]{2,1,0:T(8,128)(2,1)}) custom-call(s32[128]{0:T(128)} %bitcast.29, s32[128]{0:T(128)} %rank_ref.1, s32[128]{0:T(128)} %col_ref.1, s32[128]{0:T(128)} %row_ref.1, bf16[128,2,24,256]{3,2,1,0:T(8,128)(2,1)} %v_ref.1), custom_call_target="tpu_custom_call" | custom-call | flops 6000000000 | bytes 16000000 | tf_op jit(solution)/shard_map/pallas_call | solution.py:304
  105.6 0.0 copy-done
  105.6 7.5 %shard_map.92 = (bf16[3072,128]{1,0:T(8,128)(2,1)}, bf16[2,48,256]{2,1,0:T(8,128)(2,1)}, bf16[2,48,256]{2,1,0:T(8,128)(2,1)}) custom-call(s32[1]{0:T(128)} %bitcast.refs_0_, f32[48,1024]{1,0:T(8,128)} %bitcast.30, bf16[3072,1024]{1,0:T(8,128)(2,1)} %bitcast.31, bf16[3072,512]{1,0:T(8,128)(2,1)} %bitcast.35, bf16[3072,128]{1,0:T(8,128)(2,1)} %bitcast.39), custom_call_target="tpu_custom_call" | custom-call | flops 6000000000 | bytes 16000000 | tf_op jit(solution)/shard_map/pallas_call | solution.py:250
  113.1 8.2 %all-to-all-start = ((bf16[128,24,128]{2,1,0:T(8,128)(2,1)}), bf16[128,24,128]{2,1,0:T(8,128)(2,1)}, u32[]{:S(2)}, u32[]{:S(2)}) async-start(bf16[128,24,128]{2,1,0:T(8,128)(2,1)} %bitcast.27), calls=%async_computation | async-start | bytes 1572864 | tf_op jit(solution)/shard_map/all_to_all | solution.py:342
  121.3 3.4 %collective-permute-start.1 = (bf16[2,48,256]{2,1,0:T(8,128)(2,1)}, bf16[2,48,256]{2,1,0:T(8,128)(2,1)S(1)}, u32[]{:S(2)}, u32[]{:S(2)}) collective-permute-start(bf16[2,48,256]{2,1,0:T(8,128)(2,1)} %get-tuple-element.24.high_ref), channel_id=1, source_target_pairs={{0,2},{2,4},{4,6},{6,8},{8,10},{10,12},{12,14},{14,16},{16,18},{18... | collective-permute-start | bytes 147464 | tf_op jit(solution)/shard_map/ppermute | solution.py:354
  124.7 6.7 %collective-permute-start.2 = (bf16[2,48,256]{2,1,0:T(8,128)(2,1)}, bf16[2,48,256]{2,1,0:T(8,128)(2,1)S(1)}, u32[]{:S(2)}, u32[]{:S(2)}) collective-permute-start(bf16[2,48,256]{2,1,0:T(8,128)(2,1)} %get-tuple-element.25.low_ref), channel_id=1, source_target_pairs={{2,0},{4,2},{6,4},{8,6},{10,8},{12,10},{14,12},{16,14},{18,16},{20... | collective-permute-start | bytes 147464 | tf_op jit(solution)/shard_map/ppermute | solution.py:355
  131.4 10.2 %collective-permute-done.1.left_ref = bf16[2,48,256]{2,1,0:T(8,128)(2,1)S(1)} collective-permute-done((bf16[2,48,256]{2,1,0:T(8,128)(2,1)}, bf16[2,48,256]{2,1,0:T(8,128)(2,1)S(1)}, u32[]{:S(2)}, u32[]{:S(2)}) %collective-permute-start.1) | collective-permute-done | bytes 49184 | tf_op jit(solution)/shard_map/ppermute | solution.py:354
  141.6 0.0 copy-start.4
  141.6 0.0 collective-permute-done.2.right_ref
  141.6 0.6 copy-done.4
  142.2 0.0 copy-start.8
  142.2 0.6 copy-done.8
  142.8 5.8 %shard_map.94.refs_4_ = f32[48,1024]{1,0:T(8,128)} custom-call(s32[4,4]{1,0:T(4,128)} %offset_ref.7, bf16[2,48,256]{2,1,0:T(8,128)(2,1)} %copy-done.4, bf16[2,48,256]{2,1,0:T(8,128)(2,1)} %get-tuple-element.25.low_ref, bf16[2,48,256]{2,1,0:T(8,128)(2,1)} %get-tuple-element.24.high_ref, bf16[2,48,256]{2,1,0:T(8,128)(2,1)} %copy-done.8, ...), custom_call_target="tpu_custom_call" | custom-call | flops 3000000000 | bytes 4500000 | tf_op jit(solution)/shard_map/pallas_call | solution.py:270
  148.6 0.0 all-to-all-done
  148.6 0.0 collective-permute-done.refs_3_
  148.6 12.1 %shard_map.95 = (bf16[3072,128]{1,0:T(8,128)(2,1)}, bf16[2,48,256]{2,1,0:T(8,128)(2,1)}, bf16[2,48,256]{2,1,0:T(8,128)(2,1)}) custom-call(s32[1]{0:T(128)} %bitcast.refs_0_, bf16[3072,128]{1,0:T(8,128)(2,1)} %bitcast.7.refs_1_, bf16[3072,512]{1,0:T(8,128)(2,1)} %bitcast.17, bf16[3072,512]{1,0:T(8,128)(2,1)} %collective-permute-done.refs_3_, ...), custom_call_target="tpu_custom_call" | custom-call | flops 6000000000 | bytes 16000000 | tf_op jit(solution)/shard_map/pallas_call | solution.py:250
  160.7 9.8 %all-to-all-start.2 = ((bf16[128,24,128]{2,1,0:T(8,128)(2,1)}), bf16[128,24,128]{2,1,0:T(8,128)(2,1)S(1)}, u32[]{:S(2)}, u32[]{:S(2)}) async-start(bf16[128,24,128]{2,1,0:T(8,128)(2,1)} %bitcast.25), calls=%async_computation.2 | async-start | bytes 1572864 | tf_op jit(solution)/shard_map/all_to_all | solution.py:342
  170.5 3.4 %collective-permute-start.3 = (bf16[2,48,256]{2,1,0:T(8,128)(2,1)}, bf16[2,48,256]{2,1,0:T(8,128)(2,1)S(1)}, u32[]{:S(2)}, u32[]{:S(2)}) collective-permute-start(bf16[2,48,256]{2,1,0:T(8,128)(2,1)} %get-tuple-element.27.high_ref), channel_id=1, source_target_pairs={{0,2},{2,4},{4,6},{6,8},{8,10},{10,12},{12,14},{14,16},{16,18},{18... | collective-permute-start | bytes 147464 | tf_op jit(solution)/shard_map/ppermute | solution.py:354
  173.9 6.9 %collective-permute-start.4 = (bf16[2,48,256]{2,1,0:T(8,128)(2,1)}, bf16[2,48,256]{2,1,0:T(8,128)(2,1)S(1)}, u32[]{:S(2)}, u32[]{:S(2)}) collective-permute-start(bf16[2,48,256]{2,1,0:T(8,128)(2,1)} %get-tuple-element.28.low_ref), channel_id=1, source_target_pairs={{2,0},{4,2},{6,4},{8,6},{10,8},{12,10},{14,12},{16,14},{18,16},{20... | collective-permute-start | bytes 147464 | tf_op jit(solution)/shard_map/ppermute | solution.py:355
  180.8 9.9 %collective-permute-done.3.left_ref = bf16[2,48,256]{2,1,0:T(8,128)(2,1)S(1)} collective-permute-done((bf16[2,48,256]{2,1,0:T(8,128)(2,1)}, bf16[2,48,256]{2,1,0:T(8,128)(2,1)S(1)}, u32[]{:S(2)}, u32[]{:S(2)}) %collective-permute-start.3) | collective-permute-done | bytes 49184 | tf_op jit(solution)/shard_map/ppermute | solution.py:354
  190.6 0.0 copy-start.5
  190.6 0.0 collective-permute-done.4.right_ref
  190.6 0.6 copy-done.5
  191.2 0.0 copy-start.9
  191.2 0.6 copy-done.9
  191.9 5.8 %shard_map.96.refs_4_ = f32[48,1024]{1,0:T(8,128)} custom-call(s32[4,4]{1,0:T(4,128)} %offset_ref.7, bf16[2,48,256]{2,1,0:T(8,128)(2,1)} %copy-done.5, bf16[2,48,256]{2,1,0:T(8,128)(2,1)} %get-tuple-element.28.low_ref, bf16[2,48,256]{2,1,0:T(8,128)(2,1)} %get-tuple-element.27.high_ref, bf16[2,48,256]{2,1,0:T(8,128)(2,1)} %copy-done.9, ...), custom_call_target="tpu_custom_call" | custom-call | flops 3000000000 | bytes 4500000 | tf_op jit(solution)/shard_map/pallas_call | solution.py:270
  197.6 0.0 all-to-all-done.2
  197.6 0.0 copy-start.2
  197.6 0.9 copy-done.2
  198.5 12.1 %shard_map.97 = (bf16[3072,128]{1,0:T(8,128)(2,1)}, bf16[2,48,256]{2,1,0:T(8,128)(2,1)}, bf16[2,48,256]{2,1,0:T(8,128)(2,1)}) custom-call(s32[1]{0:T(128)} %bitcast.refs_0_, bf16[3072,128]{1,0:T(8,128)(2,1)} %bitcast.22, bf16[3072,512]{1,0:T(8,128)(2,1)} %bitcast.18, bf16[3072,512]{1,0:T(8,128)(2,1)} %collective-permute-done.refs_3_, ...), custom_call_target="tpu_custom_call" | custom-call | flops 6000000000 | bytes 16000000 | tf_op jit(solution)/shard_map/pallas_call | solution.py:250
  210.6 9.8 %all-to-all-start.3 = ((bf16[128,24,128]{2,1,0:T(8,128)(2,1)}), bf16[128,24,128]{2,1,0:T(8,128)(2,1)S(1)}, u32[]{:S(2)}, u32[]{:S(2)}) async-start(bf16[128,24,128]{2,1,0:T(8,128)(2,1)} %bitcast.26), calls=%async_computation.3 | async-start | bytes 1572864 | tf_op jit(solution)/shard_map/all_to_all | solution.py:342
  220.4 3.4 %collective-permute-start.5 = (bf16[2,48,256]{2,1,0:T(8,128)(2,1)}, bf16[2,48,256]{2,1,0:T(8,128)(2,1)S(1)}, u32[]{:S(2)}, u32[]{:S(2)}) collective-permute-start(bf16[2,48,256]{2,1,0:T(8,128)(2,1)} %get-tuple-element.30.high_ref), channel_id=1, source_target_pairs={{0,2},{2,4},{4,6},{6,8},{8,10},{10,12},{12,14},{14,16},{16,18},{18... | collective-permute-start | bytes 147464 | tf_op jit(solution)/shard_map/ppermute | solution.py:354
  223.8 6.7 %collective-permute-start.6 = (bf16[2,48,256]{2,1,0:T(8,128)(2,1)}, bf16[2,48,256]{2,1,0:T(8,128)(2,1)S(1)}, u32[]{:S(2)}, u32[]{:S(2)}) collective-permute-start(bf16[2,48,256]{2,1,0:T(8,128)(2,1)} %get-tuple-element.31.low_ref), channel_id=1, source_target_pairs={{2,0},{4,2},{6,4},{8,6},{10,8},{12,10},{14,12},{16,14},{18,16},{20... | collective-permute-start | bytes 147464 | tf_op jit(solution)/shard_map/ppermute | solution.py:355
  230.5 9.6 %collective-permute-done.5.left_ref = bf16[2,48,256]{2,1,0:T(8,128)(2,1)S(1)} collective-permute-done((bf16[2,48,256]{2,1,0:T(8,128)(2,1)}, bf16[2,48,256]{2,1,0:T(8,128)(2,1)S(1)}, u32[]{:S(2)}, u32[]{:S(2)}) %collective-permute-start.5) | collective-permute-done | bytes 49184 | tf_op jit(solution)/shard_map/ppermute | solution.py:354
  240.1 0.0 copy-start.6
  240.1 0.0 collective-permute-done.6.right_ref
  240.1 0.6 copy-done.6
  240.7 0.0 copy-start.10
  240.7 0.6 copy-done.10
  241.3 5.8 %shard_map.98.refs_4_ = f32[48,1024]{1,0:T(8,128)} custom-call(s32[4,4]{1,0:T(4,128)} %offset_ref.7, bf16[2,48,256]{2,1,0:T(8,128)(2,1)} %copy-done.6, bf16[2,48,256]{2,1,0:T(8,128)(2,1)} %get-tuple-element.31.low_ref, bf16[2,48,256]{2,1,0:T(8,128)(2,1)} %get-tuple-element.30.high_ref, bf16[2,48,256]{2,1,0:T(8,128)(2,1)} %copy-done.10, ...), custom_call_target="tpu_custom_call" | custom-call | flops 3000000000 | bytes 4500000 | tf_op jit(solution)/shard_map/pallas_call | solution.py:270
  247.1 0.0 all-to-all-done.3
  247.1 0.0 copy-start.1
  247.1 0.9 copy-done.1
  248.0 12.1 %shard_map.99 = (bf16[3072,128]{1,0:T(8,128)(2,1)}, bf16[2,48,256]{2,1,0:T(8,128)(2,1)}, bf16[2,48,256]{2,1,0:T(8,128)(2,1)}) custom-call(s32[1]{0:T(128)} %bitcast.refs_0_, bf16[3072,128]{1,0:T(8,128)(2,1)} %bitcast.21, bf16[3072,512]{1,0:T(8,128)(2,1)} %bitcast.19, bf16[3072,512]{1,0:T(8,128)(2,1)} %collective-permute-done.refs_3_, ...), custom_call_target="tpu_custom_call" | custom-call | flops 6000000000 | bytes 16000000 | tf_op jit(solution)/shard_map/pallas_call | solution.py:250
  260.1 9.9 %all-to-all-start.4 = ((bf16[128,24,128]{2,1,0:T(8,128)(2,1)}), bf16[128,24,128]{2,1,0:T(8,128)(2,1)S(1)}, u32[]{:S(2)}, u32[]{:S(2)}) async-start(bf16[128,24,128]{2,1,0:T(8,128)(2,1)} %bitcast.24), calls=%async_computation.4 | async-start | bytes 1572864 | tf_op jit(solution)/shard_map/all_to_all | solution.py:342
  270.0 3.4 %collective-permute-start.7 = (bf16[2,48,256]{2,1,0:T(8,128)(2,1)}, bf16[2,48,256]{2,1,0:T(8,128)(2,1)S(1)}, u32[]{:S(2)}, u32[]{:S(2)}) collective-permute-start(bf16[2,48,256]{2,1,0:T(8,128)(2,1)} %get-tuple-element.33.high_ref), channel_id=1, source_target_pairs={{0,2},{2,4},{4,6},{6,8},{8,10},{10,12},{12,14},{14,16},{16,18},{18... | collective-permute-start | bytes 147464 | tf_op jit(solution)/shard_map/ppermute | solution.py:354
  273.3 6.7 %collective-permute-start.8 = (bf16[2,48,256]{2,1,0:T(8,128)(2,1)}, bf16[2,48,256]{2,1,0:T(8,128)(2,1)S(1)}, u32[]{:S(2)}, u32[]{:S(2)}) collective-permute-start(bf16[2,48,256]{2,1,0:T(8,128)(2,1)} %get-tuple-element.34.low_ref), channel_id=1, source_target_pairs={{2,0},{4,2},{6,4},{8,6},{10,8},{12,10},{14,12},{16,14},{18,16},{20... | collective-permute-start | bytes 147464 | tf_op jit(solution)/shard_map/ppermute | solution.py:355
  280.0 9.3 %collective-permute-done.7.left_ref = bf16[2,48,256]{2,1,0:T(8,128)(2,1)S(1)} collective-permute-done((bf16[2,48,256]{2,1,0:T(8,128)(2,1)}, bf16[2,48,256]{2,1,0:T(8,128)(2,1)S(1)}, u32[]{:S(2)}, u32[]{:S(2)}) %collective-permute-start.7) | collective-permute-done | bytes 49184 | tf_op jit(solution)/shard_map/ppermute | solution.py:354
  289.3 0.0 copy-start.7
  289.3 0.0 collective-permute-done.8.right_ref
  289.3 0.6 copy-done.7
  289.9 0.0 copy-start.11
  289.9 0.6 copy-done.11
  290.5 5.8 %shard_map.100.refs_4_ = f32[48,1024]{1,0:T(8,128)} custom-call(s32[4,4]{1,0:T(4,128)} %offset_ref.7, bf16[2,48,256]{2,1,0:T(8,128)(2,1)} %copy-done.7, bf16[2,48,256]{2,1,0:T(8,128)(2,1)} %get-tuple-element.34.low_ref, bf16[2,48,256]{2,1,0:T(8,128)(2,1)} %get-tuple-element.33.high_ref, bf16[2,48,256]{2,1,0:T(8,128)(2,1)} %copy-done.11, ...), custom_call_target="tpu_custom_call" | custom-call | flops 3000000000 | bytes 4500000 | tf_op jit(solution)/shard_map/pallas_call | solution.py:270
  296.3 0.0 all-to-all-done.4
  296.3 0.0 copy-start.3
  296.3 0.9 copy-done.3
  297.2 5.7 %shard_map.101 = f32[48,1024]{1,0:T(8,128)} custom-call(s32[1]{0:T(128)} %bitcast.refs_0_, bf16[3072,128]{1,0:T(8,128)(2,1)} %bitcast.23, bf16[3072,512]{1,0:T(8,128)(2,1)} %bitcast.20, bf16[3072,512]{1,0:T(8,128)(2,1)} %collective-permute-done.refs_3_, f32[48,1024]{1,0:T(8,128)} %shard_map.100.refs_4_), custom_call_target="tpu_custom_call" | custom-call | flops 6000000000 | bytes 16000000 | tf_op jit(solution)/shard_map/pallas_call | solution.py:250
Async XLA Ops:
  95.1 10.4 %copy-start = (bf16[128,24,512]{2,1,0:T(8,128)(2,1)}, bf16[128,24,512]{2,1,0:T(8,128)(2,1)S(1)}, u32[]{:S(2)}) copy-start(bf16[128,24,512]{2,1,0:T(8,128)(2,1)S(1)} %all_to_all.25) | copy-start | bytes 9437188
  95.1 53.5 %collective-permute-start = (bf16[3072,512]{1,0:T(8,128)(2,1)S(1)}, bf16[3072,512]{1,0:T(8,128)(2,1)}, u32[]{:S(2)}, u32[]{:S(2)}) collective-permute-start(bf16[3072,512]{1,0:T(8,128)(2,1)S(1)} %bitcast.16), channel_id=1, source_target_pairs={{0,1},{1,0},{2,3},{3,2},{4,5},{5,4},{6,7},{7,6},{8,9},{9,8},{10,11... | collective-permute-start | bytes 9437192 | tf_op jit(solution)/shard_map/ppermute | solution.py:345
  113.1 35.5 %all-to-all-start = ((bf16[128,24,128]{2,1,0:T(8,128)(2,1)}), bf16[128,24,128]{2,1,0:T(8,128)(2,1)}, u32[]{:S(2)}, u32[]{:S(2)}) async-start(bf16[128,24,128]{2,1,0:T(8,128)(2,1)} %bitcast.27), calls=%async_computation | async-start | bytes 1572864 | tf_op jit(solution)/shard_map/all_to_all | solution.py:342
  121.3 20.3 %collective-permute-start.1 = (bf16[2,48,256]{2,1,0:T(8,128)(2,1)}, bf16[2,48,256]{2,1,0:T(8,128)(2,1)S(1)}, u32[]{:S(2)}, u32[]{:S(2)}) collective-permute-start(bf16[2,48,256]{2,1,0:T(8,128)(2,1)} %get-tuple-element.24.high_ref), channel_id=1, source_target_pairs={{0,2},{2,4},{4,6},{6,8},{8,10},{10,12},{12,14},{14,16},{16,18},{18... | collective-permute-start | bytes 147464 | tf_op jit(solution)/shard_map/ppermute | solution.py:354
  124.7 16.9 %collective-permute-start.2 = (bf16[2,48,256]{2,1,0:T(8,128)(2,1)}, bf16[2,48,256]{2,1,0:T(8,128)(2,1)S(1)}, u32[]{:S(2)}, u32[]{:S(2)}) collective-permute-start(bf16[2,48,256]{2,1,0:T(8,128)(2,1)} %get-tuple-element.25.low_ref), channel_id=1, source_target_pairs={{2,0},{4,2},{6,4},{8,6},{10,8},{12,10},{14,12},{16,14},{18,16},{20... | collective-permute-start | bytes 147464 | tf_op jit(solution)/shard_map/ppermute | solution.py:355
  141.6 0.6 copy-start.4
  142.2 0.6 copy-start.8
  160.7 36.9 %all-to-all-start.2 = ((bf16[128,24,128]{2,1,0:T(8,128)(2,1)}), bf16[128,24,128]{2,1,0:T(8,128)(2,1)S(1)}, u32[]{:S(2)}, u32[]{:S(2)}) async-start(bf16[128,24,128]{2,1,0:T(8,128)(2,1)} %bitcast.25), calls=%async_computation.2 | async-start | bytes 1572864 | tf_op jit(solution)/shard_map/all_to_all | solution.py:342
  170.5 20.1 %collective-permute-start.3 = (bf16[2,48,256]{2,1,0:T(8,128)(2,1)}, bf16[2,48,256]{2,1,0:T(8,128)(2,1)S(1)}, u32[]{:S(2)}, u32[]{:S(2)}) collective-permute-start(bf16[2,48,256]{2,1,0:T(8,128)(2,1)} %get-tuple-element.27.high_ref), channel_id=1, source_target_pairs={{0,2},{2,4},{4,6},{6,8},{8,10},{10,12},{12,14},{14,16},{16,18},{18... | collective-permute-start | bytes 147464 | tf_op jit(solution)/shard_map/ppermute | solution.py:354
  173.9 16.7 %collective-permute-start.4 = (bf16[2,48,256]{2,1,0:T(8,128)(2,1)}, bf16[2,48,256]{2,1,0:T(8,128)(2,1)S(1)}, u32[]{:S(2)}, u32[]{:S(2)}) collective-permute-start(bf16[2,48,256]{2,1,0:T(8,128)(2,1)} %get-tuple-element.28.low_ref), channel_id=1, source_target_pairs={{2,0},{4,2},{6,4},{8,6},{10,8},{12,10},{14,12},{16,14},{18,16},{20... | collective-permute-start | bytes 147464 | tf_op jit(solution)/shard_map/ppermute | solution.py:355
  190.6 0.6 copy-start.5
  191.2 0.6 copy-start.9
  197.6 0.9 copy-start.2
  210.6 36.5 %all-to-all-start.3 = ((bf16[128,24,128]{2,1,0:T(8,128)(2,1)}), bf16[128,24,128]{2,1,0:T(8,128)(2,1)S(1)}, u32[]{:S(2)}, u32[]{:S(2)}) async-start(bf16[128,24,128]{2,1,0:T(8,128)(2,1)} %bitcast.26), calls=%async_computation.3 | async-start | bytes 1572864 | tf_op jit(solution)/shard_map/all_to_all | solution.py:342
  220.4 19.6 %collective-permute-start.5 = (bf16[2,48,256]{2,1,0:T(8,128)(2,1)}, bf16[2,48,256]{2,1,0:T(8,128)(2,1)S(1)}, u32[]{:S(2)}, u32[]{:S(2)}) collective-permute-start(bf16[2,48,256]{2,1,0:T(8,128)(2,1)} %get-tuple-element.30.high_ref), channel_id=1, source_target_pairs={{0,2},{2,4},{4,6},{6,8},{8,10},{10,12},{12,14},{14,16},{16,18},{18... | collective-permute-start | bytes 147464 | tf_op jit(solution)/shard_map/ppermute | solution.py:354
  223.8 16.3 %collective-permute-start.6 = (bf16[2,48,256]{2,1,0:T(8,128)(2,1)}, bf16[2,48,256]{2,1,0:T(8,128)(2,1)S(1)}, u32[]{:S(2)}, u32[]{:S(2)}) collective-permute-start(bf16[2,48,256]{2,1,0:T(8,128)(2,1)} %get-tuple-element.31.low_ref), channel_id=1, source_target_pairs={{2,0},{4,2},{6,4},{8,6},{10,8},{12,10},{14,12},{16,14},{18,16},{20... | collective-permute-start | bytes 147464 | tf_op jit(solution)/shard_map/ppermute | solution.py:355
  240.1 0.6 copy-start.6
  240.7 0.6 copy-start.10
  247.1 0.9 copy-start.1
  260.1 36.2 %all-to-all-start.4 = ((bf16[128,24,128]{2,1,0:T(8,128)(2,1)}), bf16[128,24,128]{2,1,0:T(8,128)(2,1)S(1)}, u32[]{:S(2)}, u32[]{:S(2)}) async-start(bf16[128,24,128]{2,1,0:T(8,128)(2,1)} %bitcast.24), calls=%async_computation.4 | async-start | bytes 1572864 | tf_op jit(solution)/shard_map/all_to_all | solution.py:342
  270.0 19.3 %collective-permute-start.7 = (bf16[2,48,256]{2,1,0:T(8,128)(2,1)}, bf16[2,48,256]{2,1,0:T(8,128)(2,1)S(1)}, u32[]{:S(2)}, u32[]{:S(2)}) collective-permute-start(bf16[2,48,256]{2,1,0:T(8,128)(2,1)} %get-tuple-element.33.high_ref), channel_id=1, source_target_pairs={{0,2},{2,4},{4,6},{6,8},{8,10},{10,12},{12,14},{14,16},{16,18},{18... | collective-permute-start | bytes 147464 | tf_op jit(solution)/shard_map/ppermute | solution.py:354
  273.3 16.0 %collective-permute-start.8 = (bf16[2,48,256]{2,1,0:T(8,128)(2,1)}, bf16[2,48,256]{2,1,0:T(8,128)(2,1)S(1)}, u32[]{:S(2)}, u32[]{:S(2)}) collective-permute-start(bf16[2,48,256]{2,1,0:T(8,128)(2,1)} %get-tuple-element.34.low_ref), channel_id=1, source_target_pairs={{2,0},{4,2},{6,4},{8,6},{10,8},{12,10},{14,12},{16,14},{18,16},{20... | collective-permute-start | bytes 147464 | tf_op jit(solution)/shard_map/ppermute | solution.py:355
  289.3 0.6 copy-start.7
  289.9 0.6 copy-start.11
  296.3 0.9 copy-start.3

commit v2 on v1

v2 whole, which is shorter than its diff:
```python
import functools

import jax
import jax.numpy as jnp
from jax import lax
from jax.experimental import pallas as pl
from jax.experimental.pallas import tpu as pltpu
from jax.sharding import PartitionSpec as P

APPS = 4
BF = jnp.bfloat16
F32 = jnp.float32
VMEM_LIMIT = 20 * 1024 * 1024


def dot(a, b):
    return jnp.dot(a, b, preferred_element_type=F32)


def next_slot(count_ref, destination):
    slot = count_ref[destination]
    count_ref[destination] = slot + 1
    return slot


def clear_counts(count_ref, count):
    def body(i, carry):
        count_ref[i] = 0
        return carry

    lax.fori_loop(0, count, body, 0)


def place_u_kernel(dest_ref, u_ref, out_ref, count_ref):
    clear_counts(count_ref, out_ref.shape[0])
    out_ref[...] = jnp.zeros_like(out_ref)
    half = u_ref.shape[3]

    def body(b, carry):
        d = dest_ref[b]
        s = next_slot(count_ref, d)
        for c in range(2):
            lane = pl.multiple_of(s * (2 * half) + c * half, half)
            out_ref[d, :, pl.ds(lane, half)] = u_ref[b, c]
        return carry

    lax.fori_loop(0, u_ref.shape[0], body, 0)


def place_v_kernel(
    dest_ref, rank_ref, col_ref, row_ref, v_ref, out_ref, mask_ref, tag_ref, count_ref
):
    clear_counts(count_ref, out_ref.shape[0])
    out_ref[...] = jnp.zeros_like(out_ref)
    mask_ref[...] = jnp.zeros_like(mask_ref)
    tag_ref[...] = jnp.zeros_like(tag_ref)
    rank_size, leaf = v_ref.shape[2], v_ref.shape[3]
    group = lax.broadcasted_iota(jnp.int32, (rank_size, 256), 1) // 64
    index = lax.broadcasted_iota(jnp.int32, (rank_size, 256), 0)
    lane = lax.broadcasted_iota(jnp.int32, (rank_size, 128), 1)

    def body(b, carry):
        d = dest_ref[b]
        s = next_slot(count_ref, d)
        for c in range(2):
            at = pl.multiple_of(s * (2 * leaf) + c * leaf, leaf)
            out_ref[d, :, pl.ds(at, leaf)] = v_ref[b, c]
        kept = (group == col_ref[b]) & (index < rank_ref[b])
        mask_ref[d, :, pl.ds(pl.multiple_of(s * 256, 256), 256)] = jnp.where(kept, 1.0, 0.0).astype(
            BF
        )
        tag = jnp.where(lane == s * 64 + 48 + row_ref[b], 1.0, 0.0)
        tag_ref[d] = (tag_ref[d].astype(F32) + tag).astype(BF)
        return carry

    lax.fori_loop(0, v_ref.shape[0], body, 0)


def near_kernel(offset_ref, left_ref, low_ref, high_ref, right_ref, a_ref, out_ref, xa_ref, xb_ref):
    pad = jnp.zeros((16, 256), F32)
    for q, ref in enumerate((left_ref, low_ref, high_ref, right_ref)):
        for j in range(2):
            x = ref[j].astype(F32)
            re, im = x[:24], x[24:]
            xa_ref[q * 2 + j] = jnp.concatenate([re, im, pad], axis=0).T.astype(BF)
            xb_ref[q * 2 + j] = jnp.concatenate([-im, re, pad], axis=0).T.astype(BF)
    for i in range(a_ref.shape[0]):
        total = jnp.zeros((256, 64), F32)
        for k in range(a_ref.shape[1]):
            at = i + offset_ref[i, k] + 2
            total += dot(a_ref[i, k, 0], xa_ref[at]) + dot(a_ref[i, k, 1], xb_ref[at])
        out_ref[:, i * 256 : i * 256 + 256] = total.T[:48]


def stage_kernel(do_u, do_v, steps, *refs):
    refs = list(refs)
    core_ref = refs.pop(0)
    if do_u:
        c_ref, own_ref, other_ref, near_ref = refs[:4]
        refs = refs[4:]
        total_rows = c_ref.shape[0]
    else:
        field_ref = refs.pop(0)
    if do_v:
        v_ref, mask_ref, tag_ref = refs[:3]
        refs = refs[3:]
        total_rows = v_ref.shape[0]
        message_ref, low_ref, high_ref = refs
    else:
        (out_ref,) = refs
    rows = total_rows // steps

    if do_u:
        totals = [jnp.zeros((192, 256), F32) for w in range(2)]
        for step in range(steps):
            at = slice(step * rows, step * rows + rows)
            turned = c_ref[at].astype(F32).T
            for s in range(2):
                base = turned[s * 64 : s * 64 + 48]
                weights = jnp.concatenate(
                    [
                        (base * turned[s * 64 + 48 + o : s * 64 + 49 + o]).astype(BF)
                        for o in range(4)
                    ],
                    axis=0,
                )
                lanes = slice(s * 256, s * 256 + 256)
                totals[0] += dot(weights, own_ref[at, lanes])
                totals[1] += dot(weights, other_ref[at, lanes])
        first_core = core_ref[0] == 0
        clusters = []
        for o in range(4):
            halves = []
            for w in range(2):
                z = totals[w][o * 48 : o * 48 + 48]
                re = z[:24, :128] - z[24:, 128:]
                im = z[24:, :128] + z[:24, 128:]
                halves.append(jnp.concatenate([re, im], axis=0))
            x = jnp.concatenate(
                [
                    jnp.where(first_core, halves[0], halves[1]),
                    jnp.where(first_core, halves[1], halves[0]),
                ],
                axis=1,
            )
            clusters.append(x + near_ref[:, o * 256 : o * 256 + 256])
    else:
        clusters = [field_ref[:, m * 256 : m * 256 + 256] for m in range(4)]

    if not do_v:
        for o in range(4):
            out_ref[:, o * 256 : o * 256 + 256] = clusters[o]
        return

    pad = jnp.zeros((16, 256), F32)
    first, second = [], []
    for m, x in enumerate(clusters):
        rounded = x.astype(BF)
        (low_ref if m < 2 else high_ref)[m % 2] = rounded
        wide = rounded.astype(F32)
        re, im = wide[:24], wide[24:]
        first += [re, im, pad]
        second += [-im, re, pad]
    columns = jnp.concatenate(
        [
            jnp.concatenate(first, axis=0).T.astype(BF),
            jnp.concatenate(second, axis=0).T.astype(BF),
        ],
        axis=0,
    )
    row = lax.broadcasted_iota(jnp.int32, (512, 128), 0)
    lane = lax.broadcasted_iota(jnp.int32, (512, 128), 1)
    same = (row // 256 == lane // 64) & (row % 64 == lane % 64)
    fold = jnp.where(same, 1.0, 0.0).astype(BF)
    for step in range(steps):
        at = slice(step * rows, step * rows + rows)
        picked = []
        for s in range(2):
            p = dot(v_ref[at, s * 512 : s * 512 + 512], columns)
            picked.append(p.astype(BF) * mask_ref[at, s * 256 : s * 256 + 256])
        folded = dot(jnp.concatenate(picked, axis=1), fold)
        message_ref[at] = (folded + tag_ref[at].astype(F32)).astype(BF)


def whole_vmem(count):
    return [pl.BlockSpec(memory_space=pltpu.VMEM)] * count


SCALARS = pl.BlockSpec(memory_space=pltpu.SMEM)


def stage(do_u, do_v, core, *operands):
    if do_v:
        total_rows = operands[-1].shape[0]
        out_shape = [
            jax.ShapeDtypeStruct((total_rows, 128), BF),
            jax.ShapeDtypeStruct((2, 48, 256), BF),
            jax.ShapeDtypeStruct((2, 48, 256), BF),
        ]
        out_specs = whole_vmem(3)
    else:
        out_shape = jax.ShapeDtypeStruct((48, 1024), F32)
        out_specs = whole_vmem(1)[0]
    return pl.pallas_call(
        functools.partial(stage_kernel, do_u, do_v, 4),
        in_specs=[SCALARS] + whole_vmem(len(operands)),
        out_specs=out_specs,
        out_shape=out_shape,
        compiler_params=pltpu.CompilerParams(vmem_limit_bytes=VMEM_LIMIT),
        cost_estimate=pl.CostEstimate(
            flops=4_000_000_000, bytes_accessed=1_000_000, transcendentals=0
        ),
    )(core, *operands)


def near_call(offsets, left, low, high, right, blocks):
    return pl.pallas_call(
        near_kernel,
        in_specs=[SCALARS] + whole_vmem(5),
        out_specs=whole_vmem(1)[0],
        out_shape=jax.ShapeDtypeStruct((48, blocks.shape[0] * 256), F32),
        scratch_shapes=[pltpu.VMEM((8, 256, 64), BF), pltpu.VMEM((8, 256, 64), BF)],
        compiler_params=pltpu.CompilerParams(vmem_limit_bytes=VMEM_LIMIT),
        cost_estimate=pl.CostEstimate(
            flops=3_000_000_000, bytes_accessed=1_000_000, transcendentals=0
        ),
    )(offsets, left, low, high, right, blocks)


def place_u(dest, far_u, count):
    return pl.pallas_call(
        place_u_kernel,
        in_specs=[
            pl.BlockSpec(memory_space=pltpu.SMEM),
            pl.BlockSpec(memory_space=pltpu.VMEM),
        ],
        out_specs=pl.BlockSpec(memory_space=pltpu.VMEM),
        out_shape=jax.ShapeDtypeStruct((count, far_u.shape[2], 4 * far_u.shape[3]), BF),
        scratch_shapes=[pltpu.SMEM((count,), jnp.int32)],
        compiler_params=pltpu.CompilerParams(vmem_limit_bytes=VMEM_LIMIT),
    )(dest, far_u)


def place_v(dest, rank, col, row, far_v, count):
    rank_size, leaf = far_v.shape[2:]
    return pl.pallas_call(
        place_v_kernel,
        in_specs=[pl.BlockSpec(memory_space=pltpu.SMEM)] * 4
        + [pl.BlockSpec(memory_space=pltpu.VMEM)],
        out_specs=[pl.BlockSpec(memory_space=pltpu.VMEM)] * 3,
        out_shape=[
            jax.ShapeDtypeStruct((count, rank_size, 4 * leaf), BF),
            jax.ShapeDtypeStruct((count, rank_size, 512), BF),
            jax.ShapeDtypeStruct((count, rank_size, 128), BF),
        ],
        scratch_shapes=[pltpu.SMEM((count,), jnp.int32)],
        compiler_params=pltpu.CompilerParams(vmem_limit_bytes=VMEM_LIMIT),
        cost_estimate=pl.CostEstimate(
            flops=6_000_000_000, bytes_accessed=16_000_000, transcendentals=0
        ),
    )(dest, rank, col, row, far_v)


def on_device(
    source_field,
    near_blocks,
    near_offsets,
    far_v,
    far_u,
    far_rank,
    far_col_local,
    far_dest,
    far_row_local,
):
    parts, rhs_dev, panels_dev = source_field.shape
    rank_size = far_v.shape[2]
    count = lax.axis_size("row")
    forward = [(i, i + 1) for i in range(count - 1)]
    backward = [(i + 1, i) for i in range(count - 1)]
    core = lax.axis_index("rhs").astype(jnp.int32).reshape(1)
    dest = far_dest.reshape(-1)

    def exchange(x):
        return lax.all_to_all(x, "row", split_axis=0, concat_axis=0, tiled=True)

    u_own = exchange(place_u(dest, far_u, count))
    v_slots, mask, tag = place_v(dest, far_rank, far_col_local, far_row_local, far_v, count)
    v_slots = v_slots.reshape(count * rank_size, -1)
    mask = mask.reshape(count * rank_size, -1)
    tag = tag.reshape(count * rank_size, -1)
    message, low, high = stage(
        False, True, core, source_field.reshape(parts * rhs_dev, panels_dev), v_slots, mask, tag
    )
    for application in range(APPS):
        left = lax.ppermute(high, "row", forward)
        right = lax.ppermute(low, "row", backward)
        near_term = near_call(near_offsets, left, low, high, right, near_blocks)
        if application == 0:
            u_own, message = lax.optimization_barrier((u_own, message))
            u_own = u_own.reshape(count * rank_size, -1)
            u_other = lax.ppermute(u_own, "rhs", [(0, 1), (1, 0)])
        arrived = exchange(message.reshape(count, rank_size, 128)).reshape(-1, 128)
        if application < APPS - 1:
            message, low, high = stage(
                True, True, core, arrived, u_own, u_other, near_term, v_slots, mask, tag
            )
    result = stage(True, False, core, arrived, u_own, u_other, near_term)
    return result.reshape(parts, rhs_dev, panels_dev)


def solution(mesh):
    return jax.shard_map(
        on_device,
        mesh=mesh,
        in_specs=(
            P(None, "rhs", "row"),
            P("row", None, None, None, None),
            P("row", None),
            P("row", None, None, None),
            P("row", None, None, "rhs"),
            P("row"),
            P("row"),
            P("row", None),
            P("row"),
        ),
        out_specs=P(None, "rhs", "row"),
        check_vma=False,
    )
```

time: 305 us -> 280 us (0.918)
  blocking collectives: 89.5 us -> 0 us
  waiting for transfers between devices: 38.9 us -> 101 us
  Pallas kernels: 88.6 us -> 42.4 us
  local copies, waits for them, and re-layouts: 7.67 us -> 40.8 us
  starting transfers between devices: 78.1 us -> 94.5 us
    all_to_all x1 -> x0, blocking collectives: 89.5 us -> none  [exchange(): return lax.all_to_all(x, 'row', split_axis=0, concat_axis=0, tiled=True)]
    all_to_all x4 -> x5, waiting for transfers between devices: 0.01 us -> 61.4 us  [exchange(): return lax.all_to_all(x, 'row', split_axis=0, concat_axis=0, tiled=True)]
    pallas_call x9, Pallas kernels: 72.5 us -> 35.1 us  [the longest x5 26.4 us: stage(): pl.pallas_call(functools.partial(stage_kernel, do_u, do_v, 4), in_specs=[...]
    unnamed x24 -> x60, local copies, waits for them, and re-layouts: 7.67 us -> 40.8 us
    all_to_all x4 -> x5, starting transfers between devices: 37.7 us -> 53.6 us  [exchange(): return lax.all_to_all(x, 'row', split_axis=0, concat_axis=0, tiled=True)]
    pallas_call x1, Pallas kernels: 10.4 us -> 4.09 us  [place_v(): pl.pallas_call(place_v_kernel, in_specs=[pl.BlockSpec(memory_space=pltpu....]
  transfers between devices with their start and end apart: 13 -> 14, of which waited for: 4 -> 9; matrix products, arithmetic and copies ran while one was open for 0% -> 0% of each run, Pallas kernels for 14% -> 6%
where the time goes in v2:
time: 280 us; the launch traced here: 279 us
  waiting for transfers between devices  101 us (36%)
  starting transfers between devices  94.5 us (34%)
  Pallas kernels  42.4 us (15%)
  local copies, waits for them, and re-layouts  40.8 us (15%)
    all_to_all x5, waiting for transfers between devices, exchange(): return lax.all_to_all(x, 'row', split_axis=0, concat_axis=0, tiled=True)  61.4 us
    all_to_all x5, starting transfers between devices, exchange(): return lax.all_to_all(x, 'row', split_axis=0, concat_axis=0, tiled=True)  53.6 us
    unnamed x60, local copies, waits for them, and re-layouts  40.8 us
    ppermute x4, waiting for transfers between devices, on_device(): left = lax.ppermute(high, 'row', forward)  39.6 us
    ppermute x4, starting transfers between devices, on_device(): right = lax.ppermute(low, 'row', backward)  27.4 us
    pallas_call x5, Pallas kernels, stage(): pl.pallas_call(functools.partial(stage_kernel, do_u, do_v, 4), in_specs=[...  26.4 us
    ppermute x4, starting transfers between devices, on_device(): left = lax.ppermute(high, 'row', forward)  13.5 us
    pallas_call x4, Pallas kernels, near_call(): pl.pallas_call(near_kernel, in_specs=[SCALARS] + whole_vmem(5), out_specs...  8.78 us
  transfers between devices with their start and end apart: 14, of which 9 were waited for; matrix products, arithmetic and copies ran while one was open for 0% of the time, Pallas kernels for 6%

profile of v2, /device:TPU:32, one launch (start us, length us, event | category | flops | bytes accessed | tf_op | source)
XLA Modules:
  0.0 278.9 jit_solution(841911706356495279)
XLA Ops:
  0.0 1.4 copy-done.13
  1.4 0.7 copy-done.18
  2.1 3.2 %shard_map.91 = bf16[128,24,512]{2,1,0:T(8,128)(2,1)S(1)} custom-call(s32[128]{0:T(128)S(1)} %bitcast.37, bf16[128,2,24,128]{3,2,1,0:T(8,128)(2,1)S(1)} %copy-done.13), custom_call_target="tpu_custom_call" | custom-call | tf_op jit(solution)/shard_map/pallas_call | solution.py:231
  5.2 1.7 copy-done.8
  7.0 15.2 %all-to-all-start = ((bf16[128,24,512]{2,1,0:T(8,128)(2,1)}), bf16[128,24,512]{2,1,0:T(8,128)(2,1)S(1)}, u32[]{:S(2)}, u32[]{:S(2)}) async-start(bf16[128,24,512]{2,1,0:T(8,128)(2,1)} %copy-done.8), calls=%async_computation | async-start | bytes 6291456 | tf_op jit(solution)/shard_map/all_to_all | solution.py:284
  22.2 0.0 copy-start.24
  22.2 1.9 copy-done.24
  24.1 4.1 %shard_map.92 = (bf16[128,24,1024]{2,1,0:T(8,128)(2,1)S(1)}, bf16[128,24,512]{2,1,0:T(8,128)(2,1)S(1)}, bf16[128,24,128]{2,1,0:T(8,128)(2,1)S(1)}) custom-call(s32[128]{0:T(128)S(1)} %bitcast.38, s32[128]{0:T(128)S(1)} %copy-done.27, s32[128]{0:T(128)S(1)} %copy-done.28, s32[128]{0:T(128)S(1)} %copy-done.29, bf16[128,2,24,256]{3,2,1,0:T(8,128)(2,1)S(1)} %copy-done.24), custom_call_target="tpu_custom_call" | custom-call | flops 6000000000 | bytes 16000000 | tf_op jit(solution)/shard_map/pallas_call | solution.py:246
  28.2 0.0 copy-start.26
  28.2 2.8 %shard_map.93 = (bf16[3072,128]{1,0:T(8,128)(2,1)S(1)}, bf16[2,48,256]{2,1,0:T(8,128)(2,1)S(1)}, bf16[2,48,256]{2,1,0:T(8,128)(2,1)S(1)}) custom-call(s32[1]{0:T(128)} %bitcast.refs_0_, f32[48,1024]{1,0:T(8,128)S(1)} %bitcast.39, bf16[3072,1024]{1,0:T(8,128)(2,1)S(1)} %bitcast.16, bf16[3072,512]{1,0:T(8,128)(2,1)S(1)} %bitcast.25, bf16[3072,128]{1,0:T(8,128)(2,1)S(1)} %bitcast.29), custom_call_target="tpu_custom_call" | custom-call | flops 4000000000 | bytes 1000000 | tf_op jit(solution)/shard_map/pallas_call | solution.py:204
  31.0 2.7 copy-done
  33.7 1.7 copy-done.4
  35.5 0.9 copy-done.9
  36.3 0.9 copy-done.14
  37.2 59.4 %all-to-all-done = bf16[128,24,512]{2,1,0:T(8,128)(2,1)S(1)} async-done(((bf16[128,24,512]{2,1,0:T(8,128)(2,1)}), bf16[128,24,512]{2,1,0:T(8,128)(2,1)S(1)}, u32[]{:S(2)}, u32[]{:S(2)}) %all-to-all-start) | async-done | bytes 3145760 | tf_op jit(solution)/shard_map/all_to_all | solution.py:284
  96.6 0.0 collective-permute-start
  96.6 8.2 %all-to-all-start.1 = ((bf16[128,24,128]{2,1,0:T(8,128)(2,1)}), bf16[128,24,128]{2,1,0:T(8,128)(2,1)}, u32[]{:S(2)}, u32[]{:S(2)}) async-start(bf16[128,24,128]{2,1,0:T(8,128)(2,1)} %bitcast.33), calls=%async_computation.1 | async-start | bytes 1572864 | tf_op jit(solution)/shard_map/all_to_all | solution.py:284
  104.8 3.4 %collective-permute-start.1 = (bf16[2,48,256]{2,1,0:T(8,128)(2,1)S(1)}, bf16[2,48,256]{2,1,0:T(8,128)(2,1)S(1)}, u32[]{:S(2)}, u32[]{:S(2)}) collective-permute-start(bf16[2,48,256]{2,1,0:T(8,128)(2,1)S(1)} %get-tuple-element.28.high_ref), channel_id=1, source_target_pairs={{0,2},{2,4},{4,6},{6,8},{8,10},{10,12},{12,14},{14,16},{16,18},{18... | collective-permute-start | bytes 147464 | tf_op jit(solution)/shard_map/ppermute | solution.py:295
  108.2 6.9 %collective-permute-start.2 = (bf16[2,48,256]{2,1,0:T(8,128)(2,1)S(1)}, bf16[2,48,256]{2,1,0:T(8,128)(2,1)S(1)}, u32[]{:S(2)}, u32[]{:S(2)}) collective-permute-start(bf16[2,48,256]{2,1,0:T(8,128)(2,1)S(1)} %get-tuple-element.29.low_ref), channel_id=1, source_target_pairs={{2,0},{4,2},{6,4},{8,6},{10,8},{12,10},{14,12},{16,14},{18,16},{20... | collective-permute-start | bytes 147464 | tf_op jit(solution)/shard_map/ppermute | solution.py:296
  115.0 11.1 %collective-permute-done.1.left_ref = bf16[2,48,256]{2,1,0:T(8,128)(2,1)S(1)} collective-permute-done((bf16[2,48,256]{2,1,0:T(8,128)(2,1)S(1)}, bf16[2,48,256]{2,1,0:T(8,128)(2,1)S(1)}, u32[]{:S(2)}, u32[]{:S(2)}) %collective-permute-start.1) | collective-permute-done | bytes 49184 | tf_op jit(solution)/shard_map/ppermute | solution.py:295
  126.1 0.0 collective-permute-done.2.right_ref
  126.1 2.2 copy-done.20
  128.3 2.2 shard_map.94.refs_4_
  130.5 0.5 all-to-all-done.1
  131.0 0.0 collective-permute-done.refs_3_
  131.0 2.8 copy-done.1
  133.8 1.9 copy-done.5
  135.7 1.1 copy-done.10
  136.9 6.4 %shard_map.95 = (bf16[3072,128]{1,0:T(8,128)(2,1)S(1)}, bf16[2,48,256]{2,1,0:T(8,128)(2,1)S(1)}, bf16[2,48,256]{2,1,0:T(8,128)(2,1)S(1)}) custom-call(s32[1]{0:T(128)} %bitcast.refs_0_, bf16[3072,128]{1,0:T(8,128)(2,1)} %bitcast.7.refs_1_, bf16[3072,512]{1,0:T(8,128)(2,1)S(1)} %bitcast.21, bf16[3072,512]{1,0:T(8,128)(2,1)} %collective-permute-done.refs_3_, ...), custom_call_target="tpu_custom_call" | custom-call | flops 4000000000 | bytes 1000000 | tf_op jit(solution)/shard_map/pallas_call | solution.py:204
  143.3 0.9 copy-done.16
  144.2 10.1 %all-to-all-start.2 = ((bf16[128,24,128]{2,1,0:T(8,128)(2,1)}), bf16[128,24,128]{2,1,0:T(8,128)(2,1)}, u32[]{:S(2)}, u32[]{:S(2)}) async-start(bf16[128,24,128]{2,1,0:T(8,128)(2,1)} %bitcast.35), calls=%async_computation.2 | async-start | bytes 1572864 | tf_op jit(solution)/shard_map/all_to_all | solution.py:284
  154.3 3.4 %collective-permute-start.3 = (bf16[2,48,256]{2,1,0:T(8,128)(2,1)S(1)}, bf16[2,48,256]{2,1,0:T(8,128)(2,1)S(1)}, u32[]{:S(2)}, u32[]{:S(2)}) collective-permute-start(bf16[2,48,256]{2,1,0:T(8,128)(2,1)S(1)} %get-tuple-element.31.high_ref), channel_id=1, source_target_pairs={{0,2},{2,4},{4,6},{6,8},{8,10},{10,12},{12,14},{14,16},{16,18},{18... | collective-permute-start | bytes 147464 | tf_op jit(solution)/shard_map/ppermute | solution.py:295
  157.7 6.9 %collective-permute-start.4 = (bf16[2,48,256]{2,1,0:T(8,128)(2,1)S(1)}, bf16[2,48,256]{2,1,0:T(8,128)(2,1)S(1)}, u32[]{:S(2)}, u32[]{:S(2)}) collective-permute-start(bf16[2,48,256]{2,1,0:T(8,128)(2,1)S(1)} %get-tuple-element.32.low_ref), channel_id=1, source_target_pairs={{2,0},{4,2},{6,4},{8,6},{10,8},{12,10},{14,12},{16,14},{18,16},{20... | collective-permute-start | bytes 147464 | tf_op jit(solution)/shard_map/ppermute | solution.py:296
  164.6 10.2 %collective-permute-done.3.left_ref = bf16[2,48,256]{2,1,0:T(8,128)(2,1)S(1)} collective-permute-done((bf16[2,48,256]{2,1,0:T(8,128)(2,1)S(1)}, bf16[2,48,256]{2,1,0:T(8,128)(2,1)S(1)}, u32[]{:S(2)}, u32[]{:S(2)}) %collective-permute-start.3) | collective-permute-done | bytes 49184 | tf_op jit(solution)/shard_map/ppermute | solution.py:295
  174.8 0.0 collective-permute-done.4.right_ref
  174.8 2.2 copy-done.21
  177.0 2.2 shard_map.96.refs_4_
  179.2 0.5 all-to-all-done.2
  179.7 2.8 copy-done.2
  182.5 1.9 copy-done.6
  184.4 1.1 copy-done.11
  185.5 6.4 %shard_map.97 = (bf16[3072,128]{1,0:T(8,128)(2,1)S(1)}, bf16[2,48,256]{2,1,0:T(8,128)(2,1)S(1)}, bf16[2,48,256]{2,1,0:T(8,128)(2,1)S(1)}) custom-call(s32[1]{0:T(128)} %bitcast.refs_0_, bf16[3072,128]{1,0:T(8,128)(2,1)} %bitcast.10.refs_1_, bf16[3072,512]{1,0:T(8,128)(2,1)S(1)} %bitcast.22, bf16[3072,512]{1,0:T(8,128)(2,1)} %collective-permute-done.refs_3_, ...), custom_call_target="tpu_custom_call" | custom-call | flops 4000000000 | bytes 1000000 | tf_op jit(solution)/shard_map/pallas_call | solution.py:204
  191.9 0.9 copy-done.17
  192.8 10.1 %all-to-all-start.3 = ((bf16[128,24,128]{2,1,0:T(8,128)(2,1)}), bf16[128,24,128]{2,1,0:T(8,128)(2,1)}, u32[]{:S(2)}, u32[]{:S(2)}) async-start(bf16[128,24,128]{2,1,0:T(8,128)(2,1)} %bitcast.36), calls=%async_computation.3 | async-start | bytes 1572864 | tf_op jit(solution)/shard_map/all_to_all | solution.py:284
  202.9 3.4 %collective-permute-start.5 = (bf16[2,48,256]{2,1,0:T(8,128)(2,1)S(1)}, bf16[2,48,256]{2,1,0:T(8,128)(2,1)S(1)}, u32[]{:S(2)}, u32[]{:S(2)}) collective-permute-start(bf16[2,48,256]{2,1,0:T(8,128)(2,1)S(1)} %get-tuple-element.34.high_ref), channel_id=1, source_target_pairs={{0,2},{2,4},{4,6},{6,8},{8,10},{10,12},{12,14},{14,16},{16,18},{18... | collective-permute-start | bytes 147464 | tf_op jit(solution)/shard_map/ppermute | solution.py:295
  206.3 7.0 %collective-permute-start.6 = (bf16[2,48,256]{2,1,0:T(8,128)(2,1)S(1)}, bf16[2,48,256]{2,1,0:T(8,128)(2,1)S(1)}, u32[]{:S(2)}, u32[]{:S(2)}) collective-permute-start(bf16[2,48,256]{2,1,0:T(8,128)(2,1)S(1)} %get-tuple-element.35.low_ref), channel_id=1, source_target_pairs={{2,0},{4,2},{6,4},{8,6},{10,8},{12,10},{14,12},{16,14},{18,16},{20... | collective-permute-start | bytes 147464 | tf_op jit(solution)/shard_map/ppermute | solution.py:296
  213.3 9.4 %collective-permute-done.5.left_ref = bf16[2,48,256]{2,1,0:T(8,128)(2,1)S(1)} collective-permute-done((bf16[2,48,256]{2,1,0:T(8,128)(2,1)S(1)}, bf16[2,48,256]{2,1,0:T(8,128)(2,1)S(1)}, u32[]{:S(2)}, u32[]{:S(2)}) %collective-permute-start.5) | collective-permute-done | bytes 49184 | tf_op jit(solution)/shard_map/ppermute | solution.py:295
  222.7 0.0 collective-permute-done.6.right_ref
  222.7 2.2 copy-done.22
  224.9 2.2 shard_map.98.refs_4_
  227.1 0.5 all-to-all-done.3
  227.5 2.8 copy-done.3
  230.3 1.9 copy-done.7
  232.2 1.1 copy-done.12
  233.3 6.4 %shard_map.99 = (bf16[3072,128]{1,0:T(8,128)(2,1)S(1)}, bf16[2,48,256]{2,1,0:T(8,128)(2,1)S(1)}, bf16[2,48,256]{2,1,0:T(8,128)(2,1)S(1)}) custom-call(s32[1]{0:T(128)} %bitcast.refs_0_, bf16[3072,128]{1,0:T(8,128)(2,1)} %bitcast.12.refs_1_, bf16[3072,512]{1,0:T(8,128)(2,1)S(1)} %bitcast.23, bf16[3072,512]{1,0:T(8,128)(2,1)} %collective-permute-done.refs_3_, ...), custom_call_target="tpu_custom_call" | custom-call | flops 4000000000 | bytes 1000000 | tf_op jit(solution)/shard_map/pallas_call | solution.py:204
  239.8 0.9 copy-done.15
  240.6 10.1 %all-to-all-start.4 = ((bf16[128,24,128]{2,1,0:T(8,128)(2,1)}), bf16[128,24,128]{2,1,0:T(8,128)(2,1)}, u32[]{:S(2)}, u32[]{:S(2)}) async-start(bf16[128,24,128]{2,1,0:T(8,128)(2,1)} %bitcast.34), calls=%async_computation.4 | async-start | bytes 1572864 | tf_op jit(solution)/shard_map/all_to_all | solution.py:284
  250.7 3.4 %collective-permute-start.7 = (bf16[2,48,256]{2,1,0:T(8,128)(2,1)S(1)}, bf16[2,48,256]{2,1,0:T(8,128)(2,1)S(1)}, u32[]{:S(2)}, u32[]{:S(2)}) collective-permute-start(bf16[2,48,256]{2,1,0:T(8,128)(2,1)S(1)} %get-tuple-element.37.high_ref), channel_id=1, source_target_pairs={{0,2},{2,4},{4,6},{6,8},{8,10},{10,12},{12,14},{14,16},{16,18},{18... | collective-permute-start | bytes 147464 | tf_op jit(solution)/shard_map/ppermute | solution.py:295
  254.1 6.7 %collective-permute-start.8 = (bf16[2,48,256]{2,1,0:T(8,128)(2,1)S(1)}, bf16[2,48,256]{2,1,0:T(8,128)(2,1)S(1)}, u32[]{:S(2)}, u32[]{:S(2)}) collective-permute-start(bf16[2,48,256]{2,1,0:T(8,128)(2,1)S(1)} %get-tuple-element.38.low_ref), channel_id=1, source_target_pairs={{2,0},{4,2},{6,4},{8,6},{10,8},{12,10},{14,12},{16,14},{18,16},{20... | collective-permute-start | bytes 147464 | tf_op jit(solution)/shard_map/ppermute | solution.py:296
  260.8 9.0 %collective-permute-done.7.left_ref = bf16[2,48,256]{2,1,0:T(8,128)(2,1)S(1)} collective-permute-done((bf16[2,48,256]{2,1,0:T(8,128)(2,1)S(1)}, bf16[2,48,256]{2,1,0:T(8,128)(2,1)S(1)}, u32[]{:S(2)}, u32[]{:S(2)}) %collective-permute-start.7) | collective-permute-done | bytes 49184 | tf_op jit(solution)/shard_map/ppermute | solution.py:295
  269.7 2.2 copy-done.23
  271.9 2.2 shard_map.100.refs_4_
  274.1 0.5 all-to-all-done.4
  274.7 4.3 %shard_map.101 = f32[48,1024]{1,0:T(8,128)} custom-call(s32[1]{0:T(128)} %bitcast.refs_0_, bf16[3072,128]{1,0:T(8,128)(2,1)} %bitcast.14.refs_1_, bf16[3072,512]{1,0:T(8,128)(2,1)S(1)} %bitcast.24, bf16[3072,512]{1,0:T(8,128)(2,1)} %collective-permute-done.refs_3_, f32[48,1024]{1,0:T(8,128)S(1)} %shard_map.100.refs_4_), custom_call_target="tpu_custom_call" | custom-call | flops 4000000000 | bytes 1000000 | tf_op jit(solution)/shard_map/pallas_call | solution.py:204
  (35 shorter events, 0.1 us)
Async XLA Ops:
  0.0 1.4 copy-start.13
  1.4 0.7 copy-start.18
  5.2 1.7 copy-start.8
  6.9 15.2 %copy-start.19 = (s32[128,1]{0,1:T(1,128)S(1)}, s32[128,1]{0,1:T(1,128)}, u32[]{:S(2)}) copy-start(s32[128,1]{0,1:T(1,128)} %param.16) | copy-start | bytes 1540
  6.9 15.2 %copy-start.27 = (s32[128]{0:T(128)S(1)}, s32[128]{0:T(128)}, u32[]{:S(2)}) copy-start(s32[128]{0:T(128)} %rank_ref.1) | copy-start | bytes 1540
  6.9 15.2 %copy-start.28 = (s32[128]{0:T(128)S(1)}, s32[128]{0:T(128)}, u32[]{:S(2)}) copy-start(s32[128]{0:T(128)} %col_ref.1) | copy-start | bytes 1540
  7.0 15.2 %copy-start.29 = (s32[128]{0:T(128)S(1)}, s32[128]{0:T(128)}, u32[]{:S(2)}) copy-start(s32[128]{0:T(128)} %row_ref.1) | copy-start | bytes 1540
  7.0 89.6 %all-to-all-start = ((bf16[128,24,512]{2,1,0:T(8,128)(2,1)}), bf16[128,24,512]{2,1,0:T(8,128)(2,1)S(1)}, u32[]{:S(2)}, u32[]{:S(2)}) async-start(bf16[128,24,512]{2,1,0:T(8,128)(2,1)} %copy-done.8), calls=%async_computation | async-start | bytes 6291456 | tf_op jit(solution)/shard_map/all_to_all | solution.py:284
  22.2 1.9 copy-start.24
  24.1 4.1 %copy-start.25 = (f32[2,24,1024]{2,1,0:T(8,128)S(1)}, f32[2,24,1024]{2,1,0:T(8,128)}, u32[]{:S(2)}) copy-start(f32[2,24,1024]{2,1,0:T(8,128)} %param.9) | copy-start | bytes 589828
  28.2 98.0 %copy-start.26 = (s32[4,4]{1,0:T(4,128)S(1)}, s32[4,4]{1,0:T(4,128)}, u32[]{:S(2)}) copy-start(s32[4,4]{1,0:T(4,128)} %offset_ref.7) | copy-start | bytes 196
  31.0 2.7 copy-start
  33.7 1.7 copy-start.4
  35.5 0.9 copy-start.9
  36.3 0.9 copy-start.14
  96.6 34.5 %collective-permute-start = (bf16[3072,512]{1,0:T(8,128)(2,1)S(1)}, bf16[3072,512]{1,0:T(8,128)(2,1)}, u32[]{:S(2)}, u32[]{:S(2)}) collective-permute-start(bf16[3072,512]{1,0:T(8,128)(2,1)S(1)} %bitcast.20), channel_id=1, source_target_pairs={{0,1},{1,0},{2,3},{3,2},{4,5},{5,4},{6,7},{7,6},{8,9},{9,8},{10,11... | collective-permute-start | bytes 9437192 | tf_op jit(solution)/shard_map/ppermute | solution.py:301
  96.6 34.5 %all-to-all-start.1 = ((bf16[128,24,128]{2,1,0:T(8,128)(2,1)}), bf16[128,24,128]{2,1,0:T(8,128)(2,1)}, u32[]{:S(2)}, u32[]{:S(2)}) async-start(bf16[128,24,128]{2,1,0:T(8,128)(2,1)} %bitcast.33), calls=%async_computation.1 | async-start | bytes 1572864 | tf_op jit(solution)/shard_map/all_to_all | solution.py:284
  104.8 21.3 %collective-permute-start.1 = (bf16[2,48,256]{2,1,0:T(8,128)(2,1)S(1)}, bf16[2,48,256]{2,1,0:T(8,128)(2,1)S(1)}, u32[]{:S(2)}, u32[]{:S(2)}) collective-permute-start(bf16[2,48,256]{2,1,0:T(8,128)(2,1)S(1)} %get-tuple-element.28.high_ref), channel_id=1, source_target_pairs={{0,2},{2,4},{4,6},{6,8},{8,10},{10,12},{12,14},{14,16},{16,18},{18... | collective-permute-start | bytes 147464 | tf_op jit(solution)/shard_map/ppermute | solution.py:295
  108.2 18.0 %collective-permute-start.2 = (bf16[2,48,256]{2,1,0:T(8,128)(2,1)S(1)}, bf16[2,48,256]{2,1,0:T(8,128)(2,1)S(1)}, u32[]{:S(2)}, u32[]{:S(2)}) collective-permute-start(bf16[2,48,256]{2,1,0:T(8,128)(2,1)S(1)} %get-tuple-element.29.low_ref), channel_id=1, source_target_pairs={{2,0},{4,2},{6,4},{8,6},{10,8},{12,10},{14,12},{16,14},{18,16},{20... | collective-permute-start | bytes 147464 | tf_op jit(solution)/shard_map/ppermute | solution.py:296
  126.1 2.2 copy-start.20
  131.0 2.8 copy-start.1
  133.8 1.9 copy-start.5
  135.7 1.1 copy-start.10
  143.3 0.9 copy-start.16
  144.2 35.5 %all-to-all-start.2 = ((bf16[128,24,128]{2,1,0:T(8,128)(2,1)}), bf16[128,24,128]{2,1,0:T(8,128)(2,1)}, u32[]{:S(2)}, u32[]{:S(2)}) async-start(bf16[128,24,128]{2,1,0:T(8,128)(2,1)} %bitcast.35), calls=%async_computation.2 | async-start | bytes 1572864 | tf_op jit(solution)/shard_map/all_to_all | solution.py:284
  154.3 20.5 %collective-permute-start.3 = (bf16[2,48,256]{2,1,0:T(8,128)(2,1)S(1)}, bf16[2,48,256]{2,1,0:T(8,128)(2,1)S(1)}, u32[]{:S(2)}, u32[]{:S(2)}) collective-permute-start(bf16[2,48,256]{2,1,0:T(8,128)(2,1)S(1)} %get-tuple-element.31.high_ref), channel_id=1, source_target_pairs={{0,2},{2,4},{4,6},{6,8},{8,10},{10,12},{12,14},{14,16},{16,18},{18... | collective-permute-start | bytes 147464 | tf_op jit(solution)/shard_map/ppermute | solution.py:295
  157.7 17.1 %collective-permute-start.4 = (bf16[2,48,256]{2,1,0:T(8,128)(2,1)S(1)}, bf16[2,48,256]{2,1,0:T(8,128)(2,1)S(1)}, u32[]{:S(2)}, u32[]{:S(2)}) collective-permute-start(bf16[2,48,256]{2,1,0:T(8,128)(2,1)S(1)} %get-tuple-element.32.low_ref), channel_id=1, source_target_pairs={{2,0},{4,2},{6,4},{8,6},{10,8},{12,10},{14,12},{16,14},{18,16},{20... | collective-permute-start | bytes 147464 | tf_op jit(solution)/shard_map/ppermute | solution.py:296
  174.8 2.2 copy-start.21
  179.7 2.8 copy-start.2
  182.5 1.9 copy-start.6
  184.4 1.1 copy-start.11
  191.9 0.9 copy-start.17
  192.8 34.7 %all-to-all-start.3 = ((bf16[128,24,128]{2,1,0:T(8,128)(2,1)}), bf16[128,24,128]{2,1,0:T(8,128)(2,1)}, u32[]{:S(2)}, u32[]{:S(2)}) async-start(bf16[128,24,128]{2,1,0:T(8,128)(2,1)} %bitcast.36), calls=%async_computation.3 | async-start | bytes 1572864 | tf_op jit(solution)/shard_map/all_to_all | solution.py:284
  202.9 19.7 %collective-permute-start.5 = (bf16[2,48,256]{2,1,0:T(8,128)(2,1)S(1)}, bf16[2,48,256]{2,1,0:T(8,128)(2,1)S(1)}, u32[]{:S(2)}, u32[]{:S(2)}) collective-permute-start(bf16[2,48,256]{2,1,0:T(8,128)(2,1)S(1)} %get-tuple-element.34.high_ref), channel_id=1, source_target_pairs={{0,2},{2,4},{4,6},{6,8},{8,10},{10,12},{12,14},{14,16},{16,18},{18... | collective-permute-start | bytes 147464 | tf_op jit(solution)/shard_map/ppermute | solution.py:295
  206.3 16.4 %collective-permute-start.6 = (bf16[2,48,256]{2,1,0:T(8,128)(2,1)S(1)}, bf16[2,48,256]{2,1,0:T(8,128)(2,1)S(1)}, u32[]{:S(2)}, u32[]{:S(2)}) collective-permute-start(bf16[2,48,256]{2,1,0:T(8,128)(2,1)S(1)} %get-tuple-element.35.low_ref), channel_id=1, source_target_pairs={{2,0},{4,2},{6,4},{8,6},{10,8},{12,10},{14,12},{16,14},{18,16},{20... | collective-permute-start | bytes 147464 | tf_op jit(solution)/shard_map/ppermute | solution.py:296
  222.7 2.2 copy-start.22
  227.5 2.8 copy-start.3
  230.3 1.9 copy-start.7
  232.2 1.1 copy-start.12
  239.7 0.9 copy-start.15
  240.6 34.0 %all-to-all-start.4 = ((bf16[128,24,128]{2,1,0:T(8,128)(2,1)}), bf16[128,24,128]{2,1,0:T(8,128)(2,1)}, u32[]{:S(2)}, u32[]{:S(2)}) async-start(bf16[128,24,128]{2,1,0:T(8,128)(2,1)} %bitcast.34), calls=%async_computation.4 | async-start | bytes 1572864 | tf_op jit(solution)/shard_map/all_to_all | solution.py:284
  250.7 19.0 %collective-permute-start.7 = (bf16[2,48,256]{2,1,0:T(8,128)(2,1)S(1)}, bf16[2,48,256]{2,1,0:T(8,128)(2,1)S(1)}, u32[]{:S(2)}, u32[]{:S(2)}) collective-permute-start(bf16[2,48,256]{2,1,0:T(8,128)(2,1)S(1)} %get-tuple-element.37.high_ref), channel_id=1, source_target_pairs={{0,2},{2,4},{4,6},{6,8},{8,10},{10,12},{12,14},{14,16},{16,18},{18... | collective-permute-start | bytes 147464 | tf_op jit(solution)/shard_map/ppermute | solution.py:295
  254.1 15.7 %collective-permute-start.8 = (bf16[2,48,256]{2,1,0:T(8,128)(2,1)S(1)}, bf16[2,48,256]{2,1,0:T(8,128)(2,1)S(1)}, u32[]{:S(2)}, u32[]{:S(2)}) collective-permute-start(bf16[2,48,256]{2,1,0:T(8,128)(2,1)S(1)} %get-tuple-element.38.low_ref), channel_id=1, source_target_pairs={{2,0},{4,2},{6,4},{8,6},{10,8},{12,10},{14,12},{16,14},{18,16},{20... | collective-permute-start | bytes 147464 | tf_op jit(solution)/shard_map/ppermute | solution.py:296
  269.7 2.2 copy-start.23
